TPU v7x, 512 devices: a whole 4x8x8 slice. The times are simulated.
512 devices in a mesh: section: 8 (over x, y_lo), dp: 64 (over y_hi, z, core).
Axes of the slice: x: 4, y: 8 (y_hi: 4, y_lo: 2; y = y_hi * 2 + y_lo), z: 8, core: 2. Of those that a mesh axis runs over, the one named last changes fastest.
Arguments:
- saved: bfloat16 [8, 2, 8192, 4096], P('section', None, 'dp'), may hold values from -6 to 6
- top_grad: bfloat16 [2, 8192, 4096], P(None, 'dp'), may hold values from -0.4375 to 0.4375
- gains: float32 [8, 2, 4096], P('section'), may hold values from 0.1 to 1.9
- adapter_in: bfloat16 [8, 2, 4096, 32], P('section'), may hold values from -0.09375 to 0.09375
- adapter_out: bfloat16 [8, 2, 32, 4096], P('section'), may hold values from -1 to 1
Outputs:
- grad_in: float32 [8, 4096, 32], P('section', 'dp')
- grad_out: float32 [8, 32, 4096], P('section', None, 'dp')
All inputs are finite; a program needn't handle non-finite values.
Results may differ from a plain program's by a relative error of at most 0.014.
Values may be sent and summed in bfloat16 or wider, within the bound.
A program may use at most 64 MiB of HBM per device.

v0:
```python
from functools import partial

import jax
import jax.numpy as jnp
from jax import lax
from jax.sharding import PartitionSpec as P

EPS = 1e-05


def for_sending(shard):
    return jax.tree.map(lambda a: a.astype(jnp.bfloat16) if a.dtype == jnp.float32 else a, shard)


def passed_along(shard, axis, by):
    count = lax.axis_size(axis)
    pairs = [(i, i + by) for i in range(count) if 0 <= i + by < count]
    return lax.ppermute(shard, axis, pairs)


def from_partner(block, axis, distance):
    count = lax.axis_size(axis)
    route = []
    for low in range(count):
        high = low | 1 << distance
        if high != low and high < count:
            route += [(low, high), (high, low)]
    return lax.ppermute(block, axis, route)


def forward_part(x, gain, weight_in):
    xf = x.astype(jnp.float32)
    scale = lax.rsqrt(jnp.mean(xf * xf, axis=-1, keepdims=True) + EPS)
    normed = xf * scale
    hidden = (normed * gain).astype(jnp.bfloat16)
    pre = jnp.dot(hidden, weight_in, preferred_element_type=jnp.float32)
    return (normed, scale, hidden, pre)


def front_pass(x, gain, weight_in, weight_out, upstream):
    normed, scale, hidden, pre = forward_part(x, gain, weight_in)
    sig = jax.nn.sigmoid(pre)
    active = (pre * sig).astype(jnp.bfloat16)
    delta_act = jnp.dot(upstream, weight_out.T, preferred_element_type=jnp.float32)
    delta_pre = (delta_act * sig * (1.0 + pre * (1.0 - sig))).astype(jnp.bfloat16)
    delta_hidden = jnp.dot(delta_pre, weight_in.T, preferred_element_type=jnp.float32)
    delta_norm = delta_hidden * gain
    inner = jnp.mean(delta_norm * normed, axis=-1, keepdims=True)
    result = (upstream.astype(jnp.float32) + scale * (delta_norm - normed * inner)).astype(
        jnp.bfloat16
    )
    return (result, hidden, active, delta_pre)


def weight_terms(hidden, active, delta_pre, upstream):
    term_in = jnp.dot(hidden.T, delta_pre, preferred_element_type=jnp.float32)
    term_out = jnp.dot(active.T, upstream, preferred_element_type=jnp.float32)
    return (term_in, term_out)


def full_pass(x, gain, weight_in, weight_out, upstream):
    result, hidden, active, delta_pre = front_pass(x, gain, weight_in, weight_out, upstream)
    term_in, term_out = weight_terms(hidden, active, delta_pre, upstream)
    return (result, term_in, term_out)


def on_device(saved, top_grad, gains, adapter_in, adapter_out):
    sections = lax.axis_size("section")
    place = lax.axis_index("section")
    width = top_grad.shape[2]
    rank = adapter_in.shape[3]
    zero_in = jnp.zeros((width, rank), jnp.float32)
    zero_out = jnp.zeros((rank, width), jnp.float32)

    def pieces(replica):
        return (
            saved[0, replica],
            gains[0, replica],
            adapter_in[0, replica],
            adapter_out[0, replica],
        )

    def serves(replica, turn):
        if replica == 0:
            return place == sections - 1 - turn
        return place == turn

    def pass_on(first, second):
        moved_first = jax.tree.map(
            lambda part, own: part.astype(own.dtype),
            passed_along(for_sending(first), "section", -1),
            first,
        )
        moved_second = jax.tree.map(
            lambda part, own: part.astype(own.dtype),
            passed_along(for_sending(second), "section", 1),
            second,
        )
        return (moved_first, moved_second)

    def skip_full(upstream):
        return (upstream, zero_in, zero_out)

    def advance(turn, carry, send):
        flows = carry[0:2]
        sums = list(carry[2:])
        leaving = []
        for replica in (0, 1):
            result, term_in, term_out = lax.cond(
                serves(replica, turn),
                partial(full_pass, *pieces(replica)),
                skip_full,
                flows[replica],
            )
            leaving.append(result)
            sums[2 * replica] = sums[2 * replica] + term_in
            sums[2 * replica + 1] = sums[2 * replica + 1] + term_out
        if send:
            leaving = list(pass_on(leaving[0], leaving[1]))
        return (leaving[0], leaving[1], sums[0], sums[1], sums[2], sums[3])

    start = (top_grad[0], top_grad[1], zero_in, zero_out, zero_in, zero_out)
    carry = lax.fori_loop(0, sections - 1, lambda turn, state: advance(turn, state, True), start)
    carry = advance(sections - 1, carry, False)
    mine_in, mine_out, mirror_in, mirror_out = (carry[2], carry[3], carry[4], carry[5])
    levels = sections.bit_length() - 1
    shares = (
        lax.psum_scatter(mine_in, "dp", scatter_dimension=0, tiled=True),
        lax.psum_scatter(mine_out, "dp", scatter_dimension=1, tiled=True),
        lax.psum_scatter(mirror_in, "dp", scatter_dimension=0, tiled=True),
        lax.psum_scatter(mirror_out, "dp", scatter_dimension=1, tiled=True),
    )
    moved = (shares[2], shares[3])
    for level in range(levels):
        moved = from_partner((moved[0], moved[1]), "section", level)
    total_in = shares[0] + moved[0]
    total_out = shares[1] + moved[1]
    return (total_in[None], total_out[None])


def solution(mesh):
    in_specs = (
        P("section", None, "dp", None),
        P(None, "dp", None),
        P("section", None, None),
        P("section", None, None, None),
        P("section", None, None, None),
    )
    out_specs = (P("section", "dp", None), P("section", None, "dp"))
    return jax.shard_map(
        on_device, mesh=mesh, in_specs=in_specs, out_specs=out_specs, check_vma=False
    )
```

profile of v0, /device:TPU:57, one launch (start us, length us, event | category | flops | bytes accessed | tf_op | source)
XLA Modules:
  0.0 1005.5 jit_solution(12607118907917749522)
XLA Ops:
  7.3 2.8 slice_bitcast_fusion.4
  10.0 2.8 copy.10
  12.8 348.3 %while.30 = (s32[]{:T(128)}, bf16[128,4096]{1,0:T(8,128)(2,1)}, bf16[128,4096]{1,0:T(8,128)(2,1)S(1)}, f32[4096,32]{0,1:T(8,128)}, f32[32,4096]{1,0:T(8,128)}, /...) while((s32[]{:T(128)}, bf16[128,4096]{1,0:T(8,128)(2,1)}, ...), condition=%wide.region_9.0_spmd.clone, body=%wide.region_0.0_spmd.clone.sunk | while | flops 361873664 | bytes 59567640 | solution.py:123
  12.8 4.0 conditional.10
  12.8 2.3 copy.21
  16.8 3.0 collective-permute-start
  22.5 3.2 collective-permute-start.1
  25.8 2.3 select_add_fusion.6
  28.1 2.4 select_add_fusion.7
  30.4 13.5 %collective-permute-done = bf16[128,4096]{1,0:T(8,128)(2,1)} collective-permute-done((bf16[128,4096]{1,0:T(8,128)(2,1)}, bf16[128,4096]{1,0:T(8,128)(2,1)}, u32[]{:S(2)}, u32[]{:S(2)}) %collective-permute-start) | collective-permute-done | bytes 1048608 | tf_op jit(solution)/shard_map/while/body/eval_jaxpr/ppermute | solution.py:18
  43.9 20.4 %collective-permute-done.1 = bf16[128,4096]{1,0:T(8,128)(2,1)S(1)} collective-permute-done((bf16[128,4096]{1,0:T(8,128)(2,1)}, bf16[128,4096]{1,0:T(8,128)(2,1)S(1)}, u32[]{:S(2)}, u32[]{:S(2)}) %collective-permute-start.1) | collective-permute-done | bytes 1048608 | tf_op jit(solution)/shard_map/while/body/eval_jaxpr/ppermute | solution.py:18
  64.4 4.0 conditional.10
  64.4 2.3 copy.21
  70.3 6.8 conditional.11
  79.8 2.6 select_add_fusion.6
  82.5 2.7 select_add_fusion.7
  85.1 10.4 %collective-permute-done = bf16[128,4096]{1,0:T(8,128)(2,1)} collective-permute-done((bf16[128,4096]{1,0:T(8,128)(2,1)}, bf16[128,4096]{1,0:T(8,128)(2,1)}, u32[]{:S(2)}, u32[]{:S(2)}) %collective-permute-start) | collective-permute-done | bytes 1048608 | tf_op jit(solution)/shard_map/while/body/eval_jaxpr/ppermute | solution.py:18
  95.5 18.7 %collective-permute-done.1 = bf16[128,4096]{1,0:T(8,128)(2,1)S(1)} collective-permute-done((bf16[128,4096]{1,0:T(8,128)(2,1)}, bf16[128,4096]{1,0:T(8,128)(2,1)S(1)}, u32[]{:S(2)}, u32[]{:S(2)}) %collective-permute-start.1) | collective-permute-done | bytes 1048608 | tf_op jit(solution)/shard_map/while/body/eval_jaxpr/ppermute | solution.py:18
  114.3 4.0 conditional.10
  114.3 2.3 copy.21
  122.9 9.7 collective-permute-start.1
  132.7 2.6 select_add_fusion.6
  135.3 2.7 select_add_fusion.7
  138.0 6.7 collective-permute-done
  144.7 18.7 %collective-permute-done.1 = bf16[128,4096]{1,0:T(8,128)(2,1)S(1)} collective-permute-done((bf16[128,4096]{1,0:T(8,128)(2,1)}, bf16[128,4096]{1,0:T(8,128)(2,1)S(1)}, u32[]{:S(2)}, u32[]{:S(2)}) %collective-permute-start.1) | collective-permute-done | bytes 1048608 | tf_op jit(solution)/shard_map/while/body/eval_jaxpr/ppermute | solution.py:18
  163.5 4.0 conditional.10
  163.5 2.3 copy.21
  172.2 4.9 collective-permute-start.1
  177.1 2.6 select_add_fusion.6
  179.7 2.7 select_add_fusion.7
  182.4 11.0 %collective-permute-done = bf16[128,4096]{1,0:T(8,128)(2,1)} collective-permute-done((bf16[128,4096]{1,0:T(8,128)(2,1)}, bf16[128,4096]{1,0:T(8,128)(2,1)}, u32[]{:S(2)}, u32[]{:S(2)}) %collective-permute-start) | collective-permute-done | bytes 1048608 | tf_op jit(solution)/shard_map/while/body/eval_jaxpr/ppermute | solution.py:18
  193.3 18.7 %collective-permute-done.1 = bf16[128,4096]{1,0:T(8,128)(2,1)S(1)} collective-permute-done((bf16[128,4096]{1,0:T(8,128)(2,1)}, bf16[128,4096]{1,0:T(8,128)(2,1)S(1)}, u32[]{:S(2)}, u32[]{:S(2)}) %collective-permute-start.1) | collective-permute-done | bytes 1048608 | tf_op jit(solution)/shard_map/while/body/eval_jaxpr/ppermute | solution.py:18
  212.1 4.0 conditional.10
  212.1 2.3 copy.21
  220.7 4.9 collective-permute-start.1
  225.6 2.6 select_add_fusion.6
  228.3 2.7 select_add_fusion.7
  230.9 10.3 %collective-permute-done = bf16[128,4096]{1,0:T(8,128)(2,1)} collective-permute-done((bf16[128,4096]{1,0:T(8,128)(2,1)}, bf16[128,4096]{1,0:T(8,128)(2,1)}, u32[]{:S(2)}, u32[]{:S(2)}) %collective-permute-start) | collective-permute-done | bytes 1048608 | tf_op jit(solution)/shard_map/while/body/eval_jaxpr/ppermute | solution.py:18
  241.3 18.7 %collective-permute-done.1 = bf16[128,4096]{1,0:T(8,128)(2,1)S(1)} collective-permute-done((bf16[128,4096]{1,0:T(8,128)(2,1)}, bf16[128,4096]{1,0:T(8,128)(2,1)S(1)}, u32[]{:S(2)}, u32[]{:S(2)}) %collective-permute-start.1) | collective-permute-done | bytes 1048608 | tf_op jit(solution)/shard_map/while/body/eval_jaxpr/ppermute | solution.py:18
  260.0 4.0 conditional.10
  260.0 2.3 copy.21
  268.7 12.1 %collective-permute-start.1 = (bf16[128,4096]{1,0:T(8,128)(2,1)}, bf16[128,4096]{1,0:T(8,128)(2,1)S(1)}, u32[]{:S(2)}, u32[]{:S(2)}) collective-permute-start(bf16[128,4096]{1,0:T(8,128)(2,1)} %get-tuple-element.523), channel_id=1, source_target_pairs={{0,64},{64,128},{128,192},{192,256},{256,320},{320,384},{384,448},... | collective-permute-start | bytes 3145736 | tf_op jit(solution)/shard_map/while/body/eval_jaxpr/ppermute | solution.py:18
  280.8 2.6 select_add_fusion.6
  283.4 2.7 select_add_fusion.7
  286.1 9.7 collective-permute-done
  295.7 11.6 %collective-permute-done.1 = bf16[128,4096]{1,0:T(8,128)(2,1)S(1)} collective-permute-done((bf16[128,4096]{1,0:T(8,128)(2,1)}, bf16[128,4096]{1,0:T(8,128)(2,1)S(1)}, u32[]{:S(2)}, u32[]{:S(2)}) %collective-permute-start.1) | collective-permute-done | bytes 1048608 | tf_op jit(solution)/shard_map/while/body/eval_jaxpr/ppermute | solution.py:18
  307.3 11.2 %conditional.10 = (bf16[128,4096]{1,0:T(8,128)(2,1)}, f32[4096,32]{0,1:T(8,128)}, f32[32,4096]{1,0:T(8,128)}) conditional(s32[]{:T(128)} %convert_element_type.286, bf16[128,4096]{1,0:T(8,128)(2,1)} %get-tuple-element.560, (bf16[128,4096]{1,0:T(8,128)(2,1)}, bf16[1,2,128,4096]{3,2,1,0:T(8,128)(2,1)S(1)}, bf16[1,2,32,4096]{3,2,1,0:T(8,128)(2,1)}, ...), branch_computations={%region_1.0_spmd, %region_2.0_spmd} | conditional | flops 180412544 | bytes 21395024 | solution.py:109
  312.0 2.9 fusion.9
  316.2 2.3 fusion.33
  323.2 4.9 collective-permute-start.1
  328.1 2.6 select_add_fusion.6
  330.7 2.7 select_add_fusion.7
  333.4 9.0 collective-permute-done
  342.4 18.8 %collective-permute-done.1 = bf16[128,4096]{1,0:T(8,128)(2,1)S(1)} collective-permute-done((bf16[128,4096]{1,0:T(8,128)(2,1)}, bf16[128,4096]{1,0:T(8,128)(2,1)S(1)}, u32[]{:S(2)}, u32[]{:S(2)}) %collective-permute-start.1) | collective-permute-done | bytes 1048608 | tf_op jit(solution)/shard_map/while/body/eval_jaxpr/ppermute | solution.py:18
  368.1 3.0 copy.15
  379.2 154.8 %reduce-scatter.19.cloned.1.call-done = f32[64,32]{1,0:T(8,128)} async-done(((f32[4096,32]{1,0:T(8,128)}), f32[64,32]{1,0:T(8,128)}) %reduce-scatter.19.cloned.1.call-update) | async-done | bytes 8208
  534.8 3.0 collective-permute-start.5
  537.8 149.0 %reduce-scatter.15.cloned.1.call-done = f32[64,32]{1,0:T(8,128)} async-done(((f32[4096,32]{1,0:T(8,128)}), f32[64,32]{1,0:T(8,128)}) %reduce-scatter.15.cloned.1.call-update) | async-done | bytes 8208
  687.6 3.1 collective-permute-start.2
  690.6 3.1 collective-permute-start.6
  695.9 4.6 collective-permute-start.7
  700.6 138.2 %reduce-scatter.17.cloned.1.call-done = f32[64,32]{1,0:T(8,128)} async-done(((f32[4096,32]{1,0:T(8,128)}), f32[64,32]{1,0:T(8,128)}) %reduce-scatter.17.cloned.1.call-update) | async-done | bytes 8208
  839.6 151.9 %reduce-scatter.13.cloned.1.call-done = f32[64,32]{1,0:T(8,128)} async-done(((f32[4096,32]{1,0:T(8,128)}), f32[64,32]{1,0:T(8,128)}) %reduce-scatter.13.cloned.1.call-update) | async-done | bytes 8208
  992.4 4.6 collective-permute-start.4
  (135 shorter events, 90.0 us)
Async XLA Ops:
  7.2 526.8 %reduce-scatter.19.cloned.1.call-start = ((), (), s32[]{:S(2)}) async-start(), calls=%async_computation.7 | async-start | bytes 2129920
  10.0 2.8 copy-start
  10.0 2.8 copy-start.11
  16.8 27.1 %collective-permute-start = (bf16[128,4096]{1,0:T(8,128)(2,1)}, bf16[128,4096]{1,0:T(8,128)(2,1)}, u32[]{:S(2)}, u32[]{:S(2)}) collective-permute-start(bf16[128,4096]{1,0:T(8,128)(2,1)} %get-tuple-element.522), channel_id=1, source_target_pairs={{64,0},{128,64},{192,128},{256,192},{320,256},{384,320},{448,384},... | collective-permute-start | bytes 3145736 | tf_op jit(solution)/shard_map/while/body/eval_jaxpr/ppermute | solution.py:18
  21.7 0.8 copy-start.3
  22.5 41.8 %collective-permute-start.1 = (bf16[128,4096]{1,0:T(8,128)(2,1)}, bf16[128,4096]{1,0:T(8,128)(2,1)S(1)}, u32[]{:S(2)}, u32[]{:S(2)}) collective-permute-start(bf16[128,4096]{1,0:T(8,128)(2,1)} %get-tuple-element.523), channel_id=1, source_target_pairs={{0,64},{64,128},{128,192},{192,256},{256,320},{320,384},{384,448},... | collective-permute-start | bytes 3145736 | tf_op jit(solution)/shard_map/while/body/eval_jaxpr/ppermute | solution.py:18
  68.4 27.1 %collective-permute-start = (bf16[128,4096]{1,0:T(8,128)(2,1)}, bf16[128,4096]{1,0:T(8,128)(2,1)}, u32[]{:S(2)}, u32[]{:S(2)}) collective-permute-start(bf16[128,4096]{1,0:T(8,128)(2,1)} %get-tuple-element.522), channel_id=1, source_target_pairs={{64,0},{128,64},{192,128},{256,192},{320,256},{384,320},{448,384},... | collective-permute-start | bytes 3145736 | tf_op jit(solution)/shard_map/while/body/eval_jaxpr/ppermute | solution.py:18
  70.3 2.3 copy-start.8
  70.7 2.4 copy-start.2
  77.1 0.8 copy-start.3
  77.9 36.3 %collective-permute-start.1 = (bf16[128,4096]{1,0:T(8,128)(2,1)}, bf16[128,4096]{1,0:T(8,128)(2,1)S(1)}, u32[]{:S(2)}, u32[]{:S(2)}) collective-permute-start(bf16[128,4096]{1,0:T(8,128)(2,1)} %get-tuple-element.523), channel_id=1, source_target_pairs={{0,64},{64,128},{128,192},{192,256},{256,320},{320,384},{384,448},... | collective-permute-start | bytes 3145736 | tf_op jit(solution)/shard_map/while/body/eval_jaxpr/ppermute | solution.py:18
  118.3 26.5 %collective-permute-start = (bf16[128,4096]{1,0:T(8,128)(2,1)}, bf16[128,4096]{1,0:T(8,128)(2,1)}, u32[]{:S(2)}, u32[]{:S(2)}) collective-permute-start(bf16[128,4096]{1,0:T(8,128)(2,1)} %get-tuple-element.522), channel_id=1, source_target_pairs={{64,0},{128,64},{192,128},{256,192},{320,256},{384,320},{448,384},... | collective-permute-start | bytes 3145736 | tf_op jit(solution)/shard_map/while/body/eval_jaxpr/ppermute | solution.py:18
  122.1 0.8 copy-start.3
  122.9 40.6 %collective-permute-start.1 = (bf16[128,4096]{1,0:T(8,128)(2,1)}, bf16[128,4096]{1,0:T(8,128)(2,1)S(1)}, u32[]{:S(2)}, u32[]{:S(2)}) collective-permute-start(bf16[128,4096]{1,0:T(8,128)(2,1)} %get-tuple-element.523), channel_id=1, source_target_pairs={{0,64},{64,128},{128,192},{192,256},{256,320},{320,384},{384,448},... | collective-permute-start | bytes 3145736 | tf_op jit(solution)/shard_map/while/body/eval_jaxpr/ppermute | solution.py:18
  167.5 25.8 %collective-permute-start = (bf16[128,4096]{1,0:T(8,128)(2,1)}, bf16[128,4096]{1,0:T(8,128)(2,1)}, u32[]{:S(2)}, u32[]{:S(2)}) collective-permute-start(bf16[128,4096]{1,0:T(8,128)(2,1)} %get-tuple-element.522), channel_id=1, source_target_pairs={{64,0},{128,64},{192,128},{256,192},{320,256},{384,320},{448,384},... | collective-permute-start | bytes 3145736 | tf_op jit(solution)/shard_map/while/body/eval_jaxpr/ppermute | solution.py:18
  171.3 0.8 copy-start.3
  172.2 39.9 %collective-permute-start.1 = (bf16[128,4096]{1,0:T(8,128)(2,1)}, bf16[128,4096]{1,0:T(8,128)(2,1)S(1)}, u32[]{:S(2)}, u32[]{:S(2)}) collective-permute-start(bf16[128,4096]{1,0:T(8,128)(2,1)} %get-tuple-element.523), channel_id=1, source_target_pairs={{0,64},{64,128},{128,192},{192,256},{256,320},{320,384},{384,448},... | collective-permute-start | bytes 3145736 | tf_op jit(solution)/shard_map/while/body/eval_jaxpr/ppermute | solution.py:18
  216.1 25.2 %collective-permute-start = (bf16[128,4096]{1,0:T(8,128)(2,1)}, bf16[128,4096]{1,0:T(8,128)(2,1)}, u32[]{:S(2)}, u32[]{:S(2)}) collective-permute-start(bf16[128,4096]{1,0:T(8,128)(2,1)} %get-tuple-element.522), channel_id=1, source_target_pairs={{64,0},{128,64},{192,128},{256,192},{320,256},{384,320},{448,384},... | collective-permute-start | bytes 3145736 | tf_op jit(solution)/shard_map/while/body/eval_jaxpr/ppermute | solution.py:18
  219.9 0.8 copy-start.3
  220.7 39.3 %collective-permute-start.1 = (bf16[128,4096]{1,0:T(8,128)(2,1)}, bf16[128,4096]{1,0:T(8,128)(2,1)S(1)}, u32[]{:S(2)}, u32[]{:S(2)}) collective-permute-start(bf16[128,4096]{1,0:T(8,128)(2,1)} %get-tuple-element.523), channel_id=1, source_target_pairs={{0,64},{64,128},{128,192},{192,256},{256,320},{320,384},{384,448},... | collective-permute-start | bytes 3145736 | tf_op jit(solution)/shard_map/while/body/eval_jaxpr/ppermute | solution.py:18
  264.0 31.7 %collective-permute-start = (bf16[128,4096]{1,0:T(8,128)(2,1)}, bf16[128,4096]{1,0:T(8,128)(2,1)}, u32[]{:S(2)}, u32[]{:S(2)}) collective-permute-start(bf16[128,4096]{1,0:T(8,128)(2,1)} %get-tuple-element.522), channel_id=1, source_target_pairs={{64,0},{128,64},{192,128},{256,192},{320,256},{384,320},{448,384},... | collective-permute-start | bytes 3145736 | tf_op jit(solution)/shard_map/while/body/eval_jaxpr/ppermute | solution.py:18
  267.9 0.8 copy-start.3
  268.7 38.6 %collective-permute-start.1 = (bf16[128,4096]{1,0:T(8,128)(2,1)}, bf16[128,4096]{1,0:T(8,128)(2,1)S(1)}, u32[]{:S(2)}, u32[]{:S(2)}) collective-permute-start(bf16[128,4096]{1,0:T(8,128)(2,1)} %get-tuple-element.523), channel_id=1, source_target_pairs={{0,64},{64,128},{128,192},{192,256},{256,320},{320,384},{384,448},... | collective-permute-start | bytes 3145736 | tf_op jit(solution)/shard_map/while/body/eval_jaxpr/ppermute | solution.py:18
  307.3 2.2 copy-start.7
  307.6 3.7 copy-start.1
  318.5 23.9 %collective-permute-start = (bf16[128,4096]{1,0:T(8,128)(2,1)}, bf16[128,4096]{1,0:T(8,128)(2,1)}, u32[]{:S(2)}, u32[]{:S(2)}) collective-permute-start(bf16[128,4096]{1,0:T(8,128)(2,1)} %get-tuple-element.522), channel_id=1, source_target_pairs={{64,0},{128,64},{192,128},{256,192},{320,256},{384,320},{448,384},... | collective-permute-start | bytes 3145736 | tf_op jit(solution)/shard_map/while/body/eval_jaxpr/ppermute | solution.py:18
  322.3 0.8 copy-start.3
  323.2 38.0 %collective-permute-start.1 = (bf16[128,4096]{1,0:T(8,128)(2,1)}, bf16[128,4096]{1,0:T(8,128)(2,1)S(1)}, u32[]{:S(2)}, u32[]{:S(2)}) collective-permute-start(bf16[128,4096]{1,0:T(8,128)(2,1)} %get-tuple-element.523), channel_id=1, source_target_pairs={{0,64},{64,128},{128,192},{192,256},{256,320},{320,384},{384,448},... | collective-permute-start | bytes 3145736 | tf_op jit(solution)/shard_map/while/body/eval_jaxpr/ppermute | solution.py:18
  364.1 2.0 copy-start.6
  366.1 320.6 %reduce-scatter.15.cloned.1.call-start = ((), (), s32[]{:S(2)}) async-start(), calls=%async_computation.5 | async-start | bytes 2129920
  368.1 3.1 copy-start.9
  371.1 467.7 %reduce-scatter.17.cloned.1.call-start = ((), (), s32[]{:S(2)}) async-start(), calls=%async_computation.6 | async-start | bytes 2129920
  371.2 1.7 copy-start.5
  372.1 0.8 copy-start.10
  374.0 2.1 copy-start.4
  376.0 615.5 %reduce-scatter.13.cloned.1.call-start = ((), (), s32[]{:S(2)}) async-start(), calls=%async_computation.4 | async-start | bytes 2129920
  534.8 155.9 %collective-permute-start.5 = (f32[32,64]{1,0:T(8,128)S(1)}, f32[32,64]{1,0:T(8,128)S(1)}, u32[]{:S(2)}, u32[]{:S(2)}) collective-permute-start(f32[32,64]{1,0:T(8,128)S(1)} %copy.20), channel_id=1, source_target_pairs={{0,64},{64,0},{128,192},{192,128},{256,320},{320,256},{384,448},{4... | collective-permute-start | bytes 24584 | tf_op jit(solution)/shard_map/ppermute | solution.py:28
  687.6 6.1 collective-permute-start.2
  690.6 5.3 collective-permute-start.6
  693.7 298.7 %collective-permute-start.3 = (f32[64,32]{0,1:T(8,128)S(1)}, f32[64,32]{0,1:T(8,128)S(1)}, u32[]{:S(2)}, u32[]{:S(2)}) collective-permute-start(f32[64,32]{0,1:T(8,128)S(1)} %collective-permute-done.2), channel_id=1, source_target_pairs={{0,128},{128,0},{64,192},{192,64},{256,384},{384,256},{320,448},{4... | collective-permute-start | bytes 24584 | tf_op jit(solution)/shard_map/ppermute | solution.py:28
  695.9 301.0 %collective-permute-start.7 = (f32[32,64]{1,0:T(8,128)S(1)}, f32[32,64]{1,0:T(8,128)S(1)}, u32[]{:S(2)}, u32[]{:S(2)}) collective-permute-start(f32[32,64]{1,0:T(8,128)S(1)} %collective-permute-done.6), channel_id=1, source_target_pairs={{0,256},{256,0},{64,320},{320,64},{128,384},{384,128},{192,448},{4... | collective-permute-start | bytes 24584 | tf_op jit(solution)/shard_map/ppermute | solution.py:28
  992.4 6.0 collective-permute-start.4
Sparse Core Ops, SparseCore 0:
  366.2 167.6 reduce-scatter.18
  539.3 147.4 reduce-scatter.14
  691.4 147.3 reduce-scatter.16
  844.0 147.5 reduce-scatter.12
where the time goes:
time: 1020 us; the launch traced here: 1010 us
  waiting for transfers between devices  791 us (78%)
  starting transfers between devices  76.8 us (8%)
  local copies, waits for them, and re-layouts  62.5 us (6%)
  other arithmetic  48.3 us (5%)
  between operations  14 us (1%)
  matrix products  12.6 us (1%)
    unnamed x8, waiting for transfers between devices  594 us
    ppermute x14, waiting for transfers between devices, passed_along(): return lax.ppermute(shard, axis, pairs)  196 us
    ppermute x14, starting transfers between devices, passed_along(): return lax.ppermute(shard, axis, pairs)  56 us
    add x9, other arithmetic, advance(): sums[2 * replica] = sums[2 * replica] + term_in  21.1 us
    add x9, other arithmetic, advance(): sums[2 * replica + 1] = sums[2 * replica + 1] + term_out  20.7 us
    ppermute x6, starting transfers between devices, from_partner(): return lax.ppermute(block, axis, route)  20.6 us
  transfers between devices with their start and end apart: 24, of which 19 were waited for; matrix products, arithmetic and copies ran while one was open for 7% of the time, Pallas kernels for 0%

commit v1 on v0

v1 whole, which is shorter than its diff:
```python
from functools import partial

import jax
import jax.numpy as jnp
from jax import lax
from jax.experimental import pallas as pl
from jax.experimental.pallas import tpu as pltpu
from jax.sharding import PartitionSpec as P

EPS = 1e-05
CORES = 2
RINGS = {64: (4, 8), 8: (2, 2), 4: (1, 2)}
BF16 = jnp.bfloat16
F32 = jnp.float32


def over_last(a, b):
    return lax.dot_general(a, b, (((1,), (1,)), ((), ())), preferred_element_type=F32)


def dot(a, b):
    return jnp.dot(a, b, preferred_element_type=F32)


def kernel(
    dims, saved, top, gains, win, wout, out_in, out_out,
    xv, tv, hv, gv, iv, ov, wall, scale_v, msg, coup, got, cgot, ans, back,
    es, pe, ss, sr, fr, zs, zr, zt, yr, fin,
    load_sem, w_send, w_recv, o_send, o_recv, m_send, m_recv, k_send, k_recv,
    a_send, a_recv, c_send, c_recv, s_send, s_recv, f_send, f_recv,
    z_send, z_recv, y_send, y_recv, e_send, e_recv,
):
    S, NY, NZ, T, D, R = dims
    NL = S * R
    H = R // 2
    Q = T // S
    CH = D // NY
    me = lax.axis_index("section")
    dp = lax.axis_index("dp")
    core = lax.rem(dp, CORES)
    z = lax.rem(dp // CORES, NZ)
    yh = dp // (CORES * NZ)
    mate = dp + 1 - 2 * core
    mirror = S - 1 - me

    def on_section(j):
        return {"section": j, "dp": dp}

    def on_dp(k):
        return {"section": me, "dp": k}

    def z_peer(k):
        return yh * (NZ * CORES) + k * CORES + core

    def y_peer(k):
        return k * (NZ * CORES) + z * CORES + core

    def peer(i):
        return lax.rem(me + i, S)

    def remote(src, dst, send, recv, device):
        return pltpu.make_async_remote_copy(
            src_ref=src, dst_ref=dst, send_sem=send, recv_sem=recv,
            device_id=device, device_id_type=pl.DeviceIdType.MESH,
        )

    loads = []
    for r in range(2):
        rows = pl.ds(r * T, T)
        loads.append(pltpu.make_async_copy(saved.at[0, r], xv.at[rows], load_sem.at[r]))
    loads.append(pltpu.make_async_copy(gains.at[0], gv, load_sem.at[2]))
    loads.append(pltpu.make_async_copy(win.at[0], iv, load_sem.at[3]))
    loads.append(pltpu.make_async_copy(wout.at[0], ov, load_sem.at[4]))
    for r in range(2):
        rows = pl.ds(r * T, T)
        loads.append(pltpu.make_async_copy(top.at[r], tv.at[rows], load_sem.at[5 + r]))
    for copy in loads:
        copy.start()

    barrier = pltpu.get_barrier_semaphore()
    greeted = [on_section(peer(i)) for i in range(1, S)] + [on_dp(mate)]
    greeted += [on_dp(z_peer(lax.rem(z + i, NZ))) for i in range(1, NZ)]
    greeted += [on_dp(y_peer(lax.rem(yh + i, NY))) for i in range(1, NY)]
    for device in greeted:
        pl.semaphore_signal(barrier, inc=1, device_id=device, device_id_type=pl.DeviceIdType.MESH)
    pl.semaphore_wait(barrier, len(greeted))

    half = pl.ds(pl.multiple_of(core * H, H), H)
    other_half = pl.ds(pl.multiple_of((1 - core) * H, H), H)
    w_copies = []
    for i in range(1, S):
        j = peer(i)
        replica = jnp.where(j > me, 0, 1)
        copy = remote(
            wout.at[0, replica, half], wall.at[me, half], w_send.at[i], w_recv.at[me], on_section(j)
        )
        copy.start()
        w_copies.append(copy)

    for n in range(5):
        loads[n].wait()
    wall[me] = ov[0]

    W = 512

    def squares(i, acc):
        xf = xv[:, pl.ds(pl.multiple_of(i * 128, 128), 128)].astype(F32)
        return acc + xf * xf

    total = lax.fori_loop(0, D // 128, squares, jnp.zeros((2 * T, 128), F32), unroll=2)
    scale = lax.rsqrt(jnp.sum(total, axis=-1, keepdims=True) * (1.0 / D) + EPS)
    scale_v[...] = jnp.broadcast_to(scale, (2 * T, 128))

    def normed(i, carry):
        cols = pl.ds(pl.multiple_of(i * 128, 128), 128)
        for r in range(2):
            rows = slice(r * T, (r + 1) * T)
            nf = xv[rows, cols].astype(F32) * scale_v[rows, :]
            hv[rows, cols] = (nf * gv[r : r + 1, cols]).astype(BF16)
        return carry

    lax.fori_loop(0, D // 128, normed, 0)
    for n in range(5, 7):
        loads[n].wait()
    for r in range(2):
        rows = slice(r * T, (r + 1) * T)
        msg[:, NL + r * R : NL + (r + 1) * R] = over_last(hv[rows, :], iv[r])
        msg[:, NL + (2 + r) * R : NL + (3 + r) * R] = over_last(tv[rows, :], ov[r])
    gained = jnp.concatenate(
        [(iv[r].astype(F32) * gv[r : r + 1, :]).astype(BF16) for r in range(2)], axis=0
    )

    def fills(k, j):
        return (j != k) & ((j < k) | (j < S - 1 - k))

    for k in range(S):
        @pl.when(jnp.logical_not(fills(k, me)))
        def _():
            sr[k] = jnp.zeros((H, D), BF16)

    o_copies = []
    for i in range(1, S):
        j = peer(S - i)
        remote(wall.at[j, half], wall.at[j, half], w_send.at[i], w_recv.at[j], on_section(j)).wait_recv()
        copy = remote(wall.at[j, half], wall.at[j, half], o_send.at[i], o_recv.at[j], on_dp(mate))
        copy.start()
        o_copies.append(copy)
    for i in range(1, S):
        j = peer(S - i)
        remote(
            wall.at[j, other_half], wall.at[j, other_half], o_send.at[i], o_recv.at[j], on_dp(mate)
        ).wait_recv()

    every = wall[...].reshape(NL, D)
    through = over_last(gained, every)
    block = lax.broadcasted_iota(jnp.int32, (R, NL), 1) // R
    coup[...] = jnp.where(block < me, through[:R], through[R:]).astype(BF16)
    k_copies = []
    for i in range(1, S):
        j = peer(i)
        copy = remote(coup, cgot.at[me], k_send.at[i], k_recv.at[me], on_section(j))
        copy.start()
        k_copies.append(copy)
    cgot[me] = coup[...]

    across = over_last(xv[...], every)
    lane = lax.broadcasted_iota(jnp.int32, (T, NL), 1)
    block = lane // R
    sc0 = scale_v[:T, 0:1]
    sc1 = scale_v[T:, 0:1]
    own = jnp.where(lax.rem(lane, R) < H, sc0, sc1)
    msg[:, :NL] = jnp.where(
        block < me, across[:T] * (sc0 * sc0), jnp.where(block > me, across[T:] * (sc1 * sc1), own)
    )
    m_copies = []
    for i in range(1, S):
        j = peer(i)
        rows = pl.ds(pl.multiple_of(j * Q, Q), Q)
        copy = remote(msg.at[rows], got.at[me], m_send.at[i], m_recv.at[me], on_section(j))
        copy.start()
        m_copies.append(copy)
    got[me] = msg[pl.ds(pl.multiple_of(me * Q, Q), Q), :]
    for i in range(1, S):
        j = peer(S - i)
        remote(coup, cgot.at[j], k_send.at[i], k_recv.at[j], on_section(j)).wait_recv()
        remote(msg.at[pl.ds(0, Q)], got.at[j], m_send.at[i], m_recv.at[j], on_section(j)).wait_recv()

    pre = got[:, :, NL : NL + 2 * R]
    sig = jax.nn.sigmoid(pre)
    active = pre * sig
    slope = sig * (1.0 + pre * (1.0 - sig))
    acc = [jnp.zeros((Q, NL), F32), jnp.zeros((Q, NL), F32)]
    for turn in range(S):
        for r in range(2):
            k = S - 1 - turn if r == 0 else turn
            lanes = slice(r * R, (r + 1) * R)
            up = got[k, :, NL + (2 + r) * R : NL + (3 + r) * R]
            if turn > 0:
                up = up + acc[r][:, k * R : (k + 1) * R]
            delta = (up * slope[k, :, lanes]).astype(BF16)
            inner = jnp.sum(delta.astype(F32) * pre[k, :, lanes], axis=-1, keepdims=True) * (1.0 / D)
            ans[k, :, 2 * NL + r * R : 2 * NL + (r + 1) * R] = delta
            if turn < S - 1:
                sc = got[k, :, k * R + r * H : k * R + r * H + 1]
                acc[r] = acc[r] + sc * dot(delta, cgot[k]) - inner * got[k, :, :NL]
    for k in range(S):
        ans[0, :, k * R : (k + 1) * R] = active[k, :, :R].astype(BF16)
        ans[0, :, NL + k * R : NL + (k + 1) * R] = active[S - 1 - k, :, R:].astype(BF16)
    both = ans[0, :, : 2 * NL]
    for k in range(1, S):
        ans[k, :, : 2 * NL] = both
    a_copies = []
    mine = pl.ds(pl.multiple_of(me * Q, Q), Q)
    for i in range(1, S):
        j = peer(i)
        copy = remote(ans.at[j], back.at[me], a_send.at[i], a_recv.at[me], on_section(j))
        copy.start()
        a_copies.append(copy)
    back[me] = ans[me]
    for i in range(1, S):
        j = peer(S - i)
        remote(ans.at[j], back.at[j], a_send.at[i], a_recv.at[j], on_section(j)).wait_recv()

    answer = back[...].reshape(T, 2 * NL + 2 * R)
    block = lax.broadcasted_iota(jnp.int32, (T, NL), 1) // R
    first = answer[:, :NL].astype(F32)
    second = answer[:, NL : 2 * NL].astype(F32)
    low = jnp.concatenate(
        [jnp.where(block < me, first, 0.0), jnp.where(block < mirror, second, 0.0)], axis=0
    ).T.astype(BF16)
    same = jnp.concatenate(
        [jnp.where(block == me, first, 0.0), jnp.where(block == me, second, 0.0)], axis=0
    ).T.astype(BF16)
    deltas = [answer[:, 2 * NL + r * R : 2 * NL + (r + 1) * R] for r in range(2)]
    turned = [delta.astype(F32).T.astype(BF16) for delta in deltas]
    pulls = []
    for r in range(2):
        rows = slice(r * T, (r + 1) * T)
        pre = msg[:, NL + r * R : NL + (r + 1) * R]
        inner = jnp.sum(deltas[r].astype(F32) * pre, axis=-1, keepdims=True) * (1.0 / D)
        pulls.append(inner * scale_v[rows, 0:1])

    N = S * H
    W = min(512, CH)
    c_copies = []
    for q in range(NY):
        def part(i, carry):
            cols = pl.ds(pl.multiple_of(q * CH + i * W, W), W)
            flow = []
            for r in range(2):
                rows = slice(r * T, (r + 1) * T)
                dn = dot(deltas[r], iv[r, :, cols]) * gv[r : r + 1, cols]
                change = scale_v[rows, 0:1] * (dn - pulls[r] * xv[rows, cols].astype(F32))
                flow.append(change.astype(BF16))
                term = dot(turned[r], hv[rows, cols]).astype(BF16)
                for h in range(2):
                    es[h, N + r * H : N + (r + 1) * H, cols] = term[h * H : (h + 1) * H]
            terms = (dot(low, jnp.concatenate(flow, axis=0)) + dot(same, tv[:, cols])).astype(BF16)
            for j in range(S):
                for h in range(2):
                    es[h, j * H : (j + 1) * H, cols] = terms[j * R + h * H : j * R + (h + 1) * H]
            return carry

        lax.fori_loop(0, CH // W, part, 0)
        cols = pl.ds(q * CH, CH)
        copy = remote(es.at[1 - core, :, cols], pe.at[:, cols], c_send.at[q], c_recv.at[q], on_dp(mate))
        copy.start()
        c_copies.append(copy)

    def section_copy(i, q):
        j = peer(i)
        cols = pl.ds(q * CH, CH)
        rows = pl.ds(pl.multiple_of(j * H, H), H)
        return j, remote(
            ss.at[rows, cols], sr.at[me, :, cols], s_send.at[i, q], s_recv.at[me, q], on_section(j)
        )

    def mirror_copy(q):
        cols = pl.ds(q * CH, CH)
        return remote(
            ss.at[pl.ds(N + H, H), cols], fr.at[:, cols], f_send.at[q], f_recv.at[q], on_section(mirror)
        )

    for q in range(NY):
        cols = pl.ds(q * CH, CH)
        c_copies[q].wait_recv()
        ss[:, cols] = (es[core, :, cols].astype(F32) + pe[:, cols].astype(F32)).astype(BF16)
        for i in range(1, S):
            j, copy = section_copy(i, q)

            @pl.when(fills(me, j))
            def _():
                copy.start()
        mirror_copy(q).start()

    def z_copy(i, q):
        k = lax.rem(z + i, NZ)
        source = pl.ds(pl.multiple_of(q * CH + k * 128, 128), 128)
        return remote(
            zs.at[:, source], zr.at[z, :, pl.ds(q * 128, 128)],
            z_send.at[i, q], z_recv.at[z, q], on_dp(z_peer(k)),
        )

    for q in range(NY):
        cols = pl.ds(q * CH, CH)
        for k in range(S):
            @pl.when(fills(k, me))
            def _():
                remote(
                    ss.at[pl.ds(0, H), cols], sr.at[k, :, cols],
                    s_send.at[0, q], s_recv.at[k, q], on_section(peer(1)),
                ).wait_recv()
        mirror_copy(q).wait_recv()
        own_rows = pl.ds(pl.multiple_of(me * H, H), H)
        whole = ss[own_rows, cols].astype(F32)
        for k in range(S):
            whole = whole + sr[k, :, cols].astype(F32)
        zs[0:H, cols] = whole.astype(BF16)
        zs[H:R, cols] = (ss[N : N + H, cols].astype(F32) + fr[:, cols].astype(F32)).astype(BF16)
        for i in range(1, NZ):
            z_copy(i, q).start()
        zr[z, :, q * 128 : (q + 1) * 128] = zs[:, pl.ds(pl.multiple_of(q * CH + z * 128, 128), 128)]

    def y_copy(q):
        return remote(zt.at[q], yr.at[yh], y_send.at[q], y_recv.at[yh], on_dp(y_peer(q)))

    for q in range(NY):
        for i in range(1, NZ):
            k = lax.rem(z + i, NZ)
            remote(
                zs.at[:, pl.ds(0, 128)], zr.at[k, :, pl.ds(q * 128, 128)],
                z_send.at[i, q], z_recv.at[k, q], on_dp(z_peer(k)),
            ).wait_recv()
        whole = zr[0, :, q * 128 : (q + 1) * 128].astype(F32)
        for k in range(1, NZ):
            whole = whole + zr[k, :, q * 128 : (q + 1) * 128].astype(F32)
        zt[q] = whole

        @pl.when(yh != q)
        def _():
            y_copy(q).start()

        @pl.when(yh == q)
        def _():
            yr[q] = zt[q]

    for k in range(NY):
        @pl.when(yh != k)
        def _():
            remote(zt.at[k], yr.at[k], y_send.at[k], y_recv.at[k], on_dp(y_peer(k))).wait_recv()

    whole = yr[0]
    for k in range(1, NY):
        whole = whole + yr[k]
    fin[core] = whole
    last = remote(fin.at[core], fin.at[core], e_send.at[0], e_recv.at[0], on_dp(mate))
    last.start()
    remote(fin.at[core], fin.at[1 - core], e_send.at[0], e_recv.at[0], on_dp(mate)).wait_recv()
    for h in range(2):
        chosen = jnp.where(core == 0, fin[h, :, :64], fin[h, :, 64:])
        out_out[h * H : (h + 1) * H, :] = chosen[:H]
        out_in[h * H : (h + 1) * H, :] = chosen[H:]

    last.wait_send()
    for copy in w_copies + o_copies + k_copies + m_copies + a_copies + c_copies:
        copy.wait_send()
    for q in range(NY):
        for i in range(1, S):
            j, copy = section_copy(i, q)

            @pl.when(fills(me, j))
            def _():
                copy.wait_send()
        mirror_copy(q).wait_send()
        for i in range(1, NZ):
            z_copy(i, q).wait_send()

        @pl.when(yh != q)
        def _():
            y_copy(q).wait_send()


def on_device(rings, saved, top_grad, gains, adapter_in, adapter_out):
    S = lax.axis_size("section")
    NY, NZ = rings
    _, _, T, D = saved.shape
    R = adapter_in.shape[3]
    NL, H, Q, N = S * R, R // 2, T // S, S * (R // 2) + R
    dma = pltpu.SemaphoreType.DMA
    scratch = [
        pltpu.VMEM((2 * T, D), BF16),
        pltpu.VMEM((2 * T, D), BF16),
        pltpu.VMEM((2 * T, D), BF16),
        pltpu.VMEM((2, D), F32),
        pltpu.VMEM((2, R, D), BF16),
        pltpu.VMEM((2, R, D), BF16),
        pltpu.VMEM((S, R, D), BF16),
        pltpu.VMEM((2 * T, 128), F32),
        pltpu.VMEM((T, NL + 4 * R), F32),
        pltpu.VMEM((R, NL), BF16),
        pltpu.VMEM((S, Q, NL + 4 * R), F32),
        pltpu.VMEM((S, R, NL), BF16),
        pltpu.VMEM((S, Q, 2 * NL + 2 * R), BF16),
        pltpu.VMEM((S, Q, 2 * NL + 2 * R), BF16),
        pltpu.VMEM((2, N, D), BF16),
        pltpu.VMEM((N, D), BF16),
        pltpu.VMEM((N, D), BF16),
        pltpu.VMEM((S, H, D), BF16),
        pltpu.VMEM((H, D), BF16),
        pltpu.VMEM((R, D), BF16),
        pltpu.VMEM((NZ, R, NY * 128), BF16),
        pltpu.VMEM((NY, R, 128), F32),
        pltpu.VMEM((NY, R, 128), F32),
        pltpu.VMEM((2, R, 128), F32),
        dma((7,)),
    ]
    scratch += [dma((S,))] * 10
    scratch += [dma((NY,))] * 2
    scratch += [dma((S, NY))] * 2
    scratch += [dma((NY,))] * 2
    scratch += [dma((NZ, NY))] * 2
    scratch += [dma((NY,))] * 2
    scratch += [dma((1,))] * 2
    half = D // (NY * NZ * CORES)
    shape = jax.ShapeDtypeStruct((R, half), F32)
    grad_in, grad_out = pl.pallas_call(
        partial(kernel, (S, NY, NZ, T, D, R)),
        out_shape=(shape, shape),
        in_specs=[pl.BlockSpec(memory_space=pl.ANY)] * 5,
        out_specs=(pl.BlockSpec(memory_space=pltpu.VMEM),) * 2,
        scratch_shapes=scratch,
        compiler_params=pltpu.CompilerParams(
            collective_id=0, has_side_effects=True, vmem_limit_bytes=56 * 2**20
        ),
        cost_estimate=pl.CostEstimate(
            flops=4 * 10**9, bytes_accessed=6 * 2**20, transcendentals=2 * T * R
        ),
    )(saved, top_grad, gains, jnp.swapaxes(adapter_in, 2, 3), adapter_out)
    return (grad_in.T[None], grad_out[None])


def solution(mesh):
    in_specs = (
        P("section", None, "dp", None),
        P(None, "dp", None),
        P("section", None, None),
        P("section", None, None, None),
        P("section", None, None, None),
    )
    out_specs = (P("section", "dp", None), P("section", None, "dp"))
    return jax.shard_map(
        partial(on_device, RINGS[mesh.shape["dp"]]),
        mesh=mesh, in_specs=in_specs, out_specs=out_specs, check_vma=False,
    )
```

time: 1020 us -> 79.4 us (0.08); the launches traced: 1010 us -> 79.1 us
  waiting for transfers between devices: 791 us -> 0 us
  starting transfers between devices: 76.8 us -> 0 us
  Pallas kernels: 0 us -> 75.8 us
  local copies, waits for them, and re-layouts: 62.5 us -> 2.65 us
  other arithmetic: 48.3 us -> 0 us
  between operations: 14 us -> 0.64 us
  matrix products: 12.6 us -> 0 us
    unnamed x8 -> x0, waiting for transfers between devices: 594 us -> none
    ppermute x20 -> x0, waiting for transfers between devices: 197 us -> none  [the longest x14 196 us: passed_along(): return lax.ppermute(shard, axis, pairs)]
    ppermute x20 -> x0, starting transfers between devices: 76.6 us -> none  [the longest x14 56 us: passed_along(): return lax.ppermute(shard, axis, pairs)]
    pallas_call x0 -> x1, Pallas kernels: none -> 75.8 us  [on_device(): pl.pallas_call(partial(kernel, (S, NY, NZ, T, D, R)), out_shape=(shape, s...]
    add x18 -> x0, other arithmetic: 41.9 us -> none  [the longest x9 21.1 us: advance(): sums[2 * replica] = sums[2 * replica] + term_in]
    cond x20 -> x0, local copies, waits for them, and re-layouts: 19.8 us -> none
    broadcast_in_dim x28 -> x0, local copies, waits for them, and re-layouts: 18.3 us -> none  [the longest x14 11.2 us: on_device(): zero_out = jnp.zeros((rank, width), jnp.float32)]
    unnamed x23 -> x2, local copies, waits for them, and re-layouts: 15.8 us -> 2.65 us
  transfers between devices with their start and end apart: 24 -> 0, of which waited for: 19 -> 0; matrix products, arithmetic and copies ran while one was open for 7% -> 0% of each run, Pallas kernels for 0% -> 0%
where the time goes in v1:
time: 79.4 us; the launch traced here: 79.1 us
  Pallas kernels  75.8 us (95%)
  local copies, waits for them, and re-layouts  2.65 us (3%)
    pallas_call x1, Pallas kernels, on_device(): pl.pallas_call(partial(kernel, (S, NY, NZ, T, D, R)), out_shape=(shape, s...  75.8 us
    unnamed x2, local copies, waits for them, and re-layouts  2.65 us

profile of v1, /device:TPU:57, one launch (start us, length us, event | category | flops | bytes accessed | tf_op | source)
XLA Modules:
  0.0 79.1 jit_solution(8247847476697906420)
XLA Ops:
  0.6 75.8 %shard_map.68 = (f32[32,64]{1,0:T(8,128)}, f32[32,64]{1,0:T(8,128)}) custom-call(bf16[1,2,128,4096]{3,2,1,0:T(8,128)(2,1)} %saved.1, bf16[2,128,4096]{2,1,0:T(8,128)(2,1)} %top.1, f32[1,2,4096]{2,1,0:T(2,128)} %gains.1, bf16[1,2,32,4096]{3,2,1,0:T(8,128)(2,1)} %bitcast.7, bf16[1,2,32,4096]{3,2,1,0:T(8,128)(2,1)} %wout.1), custom_call_target="tpu_custom_call" | custom-call | flops 4000000000 | bytes 6291456 | tf_op jit(solution)/shard_map/pallas_call | solution.py:426
  76.5 1.3 %copy.9 = f32[1,64,32]{1,2,0:T(8,128)} copy(f32[1,64,32]{1,2,0:T(8,128)} %bitcast.6) | data formatting | bytes 16384
  77.8 1.3 %copy.10 = f32[1,32,64]{2,1,0:T(8,128)} copy(f32[1,32,64]{2,1,0:T(8,128)} %bitcast.5) | data formatting | bytes 16384

commit v2 on v0

v2 whole, which is shorter than its diff:
```python
from functools import partial

import jax
import jax.numpy as jnp
from jax import lax
from jax.experimental import pallas as pl
from jax.experimental.pallas import tpu as pltpu
from jax.sharding import PartitionSpec as P

EPS = 1e-05
CORES = 2
RINGS = {64: (4, 8), 8: (2, 2), 4: (1, 2)}
BF16 = jnp.bfloat16
F32 = jnp.float32


def over_last(a, b):
    return lax.dot_general(a, b, (((1,), (1,)), ((), ())), preferred_element_type=F32)


def dot(a, b):
    return jnp.dot(a, b, preferred_element_type=F32)


def kernel(
    dims, saved, top, gains, win, wout, out,
    lhs, tv, hv, gv, iv, ov, wall, scale_v, scale_t, pre_v, pre_t, mix, early, late, coup, egot, lgot, cgot,
    act_t, low, same, ans, back, own_s, own_r, ds, dr, es, pe, ss, yb, xs, xr, fr, zs, zr, zt, yr,
    load_sem, wx_send, wx_recv, wd_send, wd_recv, wy_send, wy_recv, wc_send, wc_recv,
    e_send, e_recv, t_send, t_recv, g_send, g_recv, v_send, v_recv, k_send, k_recv,
    a_send, a_recv, o_send, o_recv, d_send, d_recv, c_send, c_recv, ty_send, ty_recv, tx_send, tx_recv, f_send, f_recv,
    z_send, z_recv, y_send, y_recv,
):
    S, NY, NZ, T, D, R = dims
    X = S // 2
    NL = S * R
    H = R // 2
    Q = T // S
    CH = D // NY
    me = lax.axis_index("section")
    dp = lax.axis_index("dp")
    x = me // 2
    yl = lax.rem(me, 2)
    core = lax.rem(dp, CORES)
    z = lax.rem(dp // CORES, NZ)
    yh = dp // (CORES * NZ)
    mate = dp + 1 - 2 * core
    mirror = S - 1 - me
    far = lax.rem(yh + 2 * yl + NY - 1, NY)
    NEAR = 128 * (3 * CH // 1024) if CH >= 1024 else CH // 2
    beside = 2 * x + 1 - yl

    def on_section(j):
        return {"section": j, "dp": dp}

    def on_dp(k):
        return {"section": me, "dp": k}

    def place(h, k, c=None):
        return h * (NZ * CORES) + k * CORES + (core if c is None else c)

    def y_next(way):
        return {"section": beside, "dp": dp if way == 0 else place(far, z)}

    def side(q, way):
        return pl.ds(q * CH, NEAR) if way == 0 else pl.ds(q * CH + NEAR, CH - NEAR)

    def peer(i):
        return lax.rem(me + i, S)

    def x_peer(i):
        return lax.rem(x + i, X)

    def in_row(k):
        return on_section(2 * k + yl)

    def remote(src, dst, send, recv, device):
        return pltpu.make_async_remote_copy(
            src_ref=src, dst_ref=dst, send_sem=send, recv_sem=recv,
            device_id=device, device_id_type=pl.DeviceIdType.MESH,
        )

    sent = []

    def go(copy):
        copy.start()
        sent.append(copy)

    def chunk(q):
        return pl.ds(q * CH, CH)

    half = pl.ds(pl.multiple_of(core * H, H), H)
    other_half = pl.ds(pl.multiple_of((1 - core) * H, H), H)
    steps_of = [(0, 1)] + [(dx, dy) for dx in sorted(range(1, X), key=lambda n: min(n, X - n)) for dy in range(2)]

    def section_at(dx, dy, sign=1):
        return 2 * lax.rem(x + X + sign * dx, X) + (1 - yl if dy else yl)

    own_unit = pltpu.make_async_copy(wout.at[0, yl, half], wall.at[x, yl, half], load_sem.at[7])
    own_unit.start()

    loads = []
    for r in range(2):
        rows = pl.ds(r * T, T)
        loads.append(pltpu.make_async_copy(saved.at[0, r], lhs.at[rows], load_sem.at[r]))
    loads.append(pltpu.make_async_copy(gains.at[0], gv, load_sem.at[2]))
    loads.append(pltpu.make_async_copy(win.at[0], iv, load_sem.at[3]))
    loads.append(pltpu.make_async_copy(wout.at[0], ov, load_sem.at[4]))
    for r in range(2):
        rows = pl.ds(r * T, T)
        loads.append(pltpu.make_async_copy(top.at[r], tv.at[rows], load_sem.at[5 + r]))
    for copy in loads:
        copy.start()

    barrier = pltpu.get_barrier_semaphore()
    greeted = [on_section(peer(i)) for i in range(1, S)] + [on_dp(mate)]
    greeted += [{"section": beside, "dp": place(far, z)}]
    greeted += [on_dp(place(yh, lax.rem(z + i, NZ))) for i in range(1, NZ)]
    greeted += [on_dp(place(lax.rem(yh + i, NY), z, c)) for i in range(1, NY) for c in range(CORES)]
    for device in greeted:
        pl.semaphore_signal(barrier, inc=1, device_id=device, device_id_type=pl.DeviceIdType.MESH)
    pl.semaphore_wait(barrier, len(greeted))

    near = pl.ds(0, D // 2)
    rest = pl.ds(D // 2, D // 2)

    def upper(j):
        return jnp.where(j > me, 0, 1)

    rows_sent = []
    for i in range(1, X):
        j = 2 * x_peer(i) + yl
        copy = remote(
            wout.at[0, upper(j), half, near], wall.at[x, yl, half, near], wx_send.at[i], wx_recv.at[x], on_section(j)
        )
        copy.start()
        rows_sent.append(copy)

    def send_direct():
        for copy in rows_sent:
            copy.wait_send()
        for n, (dx, dy) in reversed(list(enumerate(steps_of))):
            j = section_at(dx, dy)
            go(remote(
                wout.at[0, upper(j), half, rest], wall.at[x, yl, half, rest],
                wd_send.at[n], wd_recv.at[me], on_section(j),
            ))

    for j in range(S):
        @pl.when(j >= me)
        def _():
            low[j * R : (j + 1) * R, 0:T] = jnp.zeros((R, T), BF16)

        @pl.when(j >= mirror)
        def _():
            low[j * R : (j + 1) * R, T : 2 * T] = jnp.zeros((R, T), BF16)

    xr[x] = jnp.zeros((H, D), BF16)

    def onward(way):
        return pl.ds(way * (D // 4), D // 4)

    def gather_row():
        own_unit.wait()
        for i in range(1, X):
            k = x_peer(X - i)
            landed = wall.at[k, yl, half, near]
            remote(landed, landed, wx_send.at[i], wx_recv.at[k], in_row(k)).wait_recv()
        for way in range(2):
            row = wall.at[:, yl, half, onward(way)]
            go(remote(row, row, wy_send.at[way], wy_recv.at[way], y_next(way)))
        row = wall.at[:, yl, half, near]
        go(remote(row, row, wc_send.at[0], wc_recv.at[0], on_dp(mate)))

    def gather_y():
        for way in range(2):
            row = wall.at[:, 1 - yl, half, onward(way)]
            remote(row, row, wy_send.at[way], wy_recv.at[way], y_next(way)).wait_recv()
        row = wall.at[:, 1 - yl, half, near]
        go(remote(row, row, wc_send.at[1], wc_recv.at[1], on_dp(mate)))

    def gather_direct():
        for n, (dx, dy) in enumerate(steps_of):
            j = section_at(dx, dy, -1)
            landed = wall.at[j // 2, lax.rem(j, 2), half, rest]
            remote(landed, landed, wd_send.at[n], wd_recv.at[j], on_section(j)).wait_recv()
        row = wall.at[:, :, half, rest]
        go(remote(row, row, wc_send.at[2], wc_recv.at[2], on_dp(mate)))

    def project_near():
        for n, line in enumerate((yl, 1 - yl)):
            row = wall.at[:, line, other_half, near]
            remote(row, row, wc_send.at[n], wc_recv.at[n], on_dp(mate)).wait_recv()
        return over_last(lhs[:, : D // 2], wall[:, :, :, : D // 2].reshape(NL, D // 2))

    def project_rest():
        row = wall.at[:, :, other_half, rest]
        remote(row, row, wc_send.at[2], wc_recv.at[2], on_dp(mate)).wait_recv()
        return over_last(lhs[:, D // 2 :], wall[:, :, :, D // 2 :].reshape(NL, D // 2))

    def piece_norm():
        for n in range(2):
            loads[n].wait()

        def squares(i, acc):
            xf = lhs[0 : 2 * T, pl.ds(pl.multiple_of(i * 128, 128), 128)].astype(F32)
            return acc + xf * xf

        total = lax.fori_loop(0, D // 128, squares, jnp.zeros((2 * T, 128), F32), unroll=2)
        scale = lax.rsqrt(jnp.sum(total, axis=-1, keepdims=True) * (1.0 / D) + EPS)
        wide = jnp.broadcast_to(scale, (2 * T, 128))
        scale_v[...] = wide
        scale_t[...] = wide.T[0:8]

    def piece_hidden():
        for n in range(2, 5):
            loads[n].wait()

        def normed(i, carry):
            cols = pl.ds(pl.multiple_of(i * 128, 128), 128)
            for r in range(2):
                rows = slice(r * T, (r + 1) * T)
                nf = lhs[rows, cols].astype(F32) * scale_v[rows, :]
                hv[rows, cols] = (nf * gv[r : r + 1, cols]).astype(BF16)
                lhs[2 * T + r * R : 2 * T + (r + 1) * R, cols] = (
                    iv[r, :, cols].astype(F32) * gv[r : r + 1, cols]
                ).astype(BF16)
            return carry

        lax.fori_loop(0, D // 128, normed, 0)

    def piece_down():
        for r in range(2):
            rows = slice(r * T, (r + 1) * T)
            pre = over_last(hv[rows, :], iv[r])
            pre_v[:, r * R : (r + 1) * R] = pre
            early[:, r * R : (r + 1) * R] = pre
        pre = pre_v[...].T
        pre_t[...] = pre
        active = pre * jax.nn.sigmoid(pre)
        for r in range(2):
            act_t[r] = active[r * R : (r + 1) * R].astype(BF16)
        same[:, 0:T] = act_t[0]
        for i in range(1, S):
            j = peer(i)
            replica = jnp.where(j > me, 0, 1)
            rows = pl.ds(pl.multiple_of(jnp.where(j > me, me, mirror) * R, R), R)
            lanes = pl.ds(pl.multiple_of(replica * T, T), T)
            go(remote(act_t.at[replica], low.at[rows, lanes], t_send.at[i], t_recv.at[me], on_section(j)))
        go(remote(act_t.at[1], same.at[:, pl.ds(T, T)], g_send.at[0], g_recv.at[0], on_section(mirror)))

    def piece_up():
        for n in range(5, 7):
            loads[n].wait()
        for r in range(2):
            rows = slice(r * T, (r + 1) * T)
            early[:, (2 + r) * R : (3 + r) * R] = over_last(tv[rows, :], ov[r])
        for i in range(1, S):
            j = peer(i)
            rows = pl.ds(pl.multiple_of(j * Q, Q), Q)
            go(remote(early.at[rows], egot.at[me], e_send.at[i], e_recv.at[me], on_section(j)))
        egot[me] = early[pl.ds(pl.multiple_of(me * Q, Q), Q), :]

    piece_norm()
    send_direct()
    piece_hidden()
    gather_row()
    piece_down()
    piece_up()
    gather_y()
    gather_direct()
    across = project_near() + project_rest()

    block = lax.broadcasted_iota(jnp.int32, (R, NL), 1) // R
    coup[...] = jnp.where(
        block < me, across[2 * T : 2 * T + R], across[2 * T + R :]
    ).astype(BF16)
    lane = lax.broadcasted_iota(jnp.int32, (T, NL), 1)
    block = lane // R
    within = lax.rem(lane, R) // (R // 4)
    sc0 = scale_v[:T, 0:1]
    sc1 = scale_v[T:, 0:1]
    sc = jnp.where(within < 2, sc0, sc1)
    rounded = sc.astype(BF16).astype(F32)
    own = jnp.where(lax.rem(within, 2) == 0, rounded, sc - rounded)
    late[...] = jnp.where(
        block < me, across[:T] * (sc0 * sc0), jnp.where(block > me, across[T : 2 * T] * (sc1 * sc1), own)
    ).astype(BF16)
    for i in range(1, S):
        j = peer(i)
        rows = pl.ds(pl.multiple_of(j * Q, Q), Q)
        go(remote(coup, cgot.at[me], k_send.at[i], k_recv.at[me], on_section(j)))
        go(remote(late.at[rows], lgot.at[me], v_send.at[i], v_recv.at[me], on_section(j)))
    cgot[me] = coup[...]
    lgot[me] = late[pl.ds(pl.multiple_of(me * Q, Q), Q), :]

    remote(act_t.at[1], same.at[:, pl.ds(T, T)], g_send.at[0], g_recv.at[0], on_section(mirror)).wait_recv()
    for q in range(NY):
        term = dot(same[...], tv[:, chunk(q)])
        for h in range(2):
            own_s[h, :, chunk(q)] = term[h * H : (h + 1) * H]
    go(remote(own_s.at[1 - core], own_r, o_send.at[0], o_recv.at[0], on_dp(mate)))

    for i in range(1, S):
        j = peer(S - i)
        remote(early.at[pl.ds(0, Q)], egot.at[j], e_send.at[i], e_recv.at[j], on_section(j)).wait_recv()
    pre = egot[:, :, 0 : 2 * R]
    sig = jax.nn.sigmoid(pre)
    slope = sig * (1.0 + pre * (1.0 - sig))
    for i in range(1, S):
        j = peer(S - i)
        remote(coup, cgot.at[j], k_send.at[i], k_recv.at[j], on_section(j)).wait_recv()
        remote(late.at[pl.ds(0, Q)], lgot.at[j], v_send.at[i], v_recv.at[j], on_section(j)).wait_recv()

    acc = [jnp.zeros((Q, NL), F32), jnp.zeros((Q, NL), F32)]
    for turn in range(S):
        for r in range(2):
            k = S - 1 - turn if r == 0 else turn
            lanes = slice(r * R, (r + 1) * R)
            up = egot[k, :, (2 + r) * R : (3 + r) * R]
            if turn > 0:
                up = up + acc[r][:, k * R : (k + 1) * R]
            delta = (up * slope[k, :, lanes]).astype(BF16)
            ans[k, :, lanes] = delta
            if turn < S - 1:
                inner = jnp.sum(delta.astype(F32) * pre[k, :, lanes], axis=-1, keepdims=True) * (1.0 / D)
                first = k * R + r * H
                sc = lgot[k, :, first : first + 1].astype(F32)
                sc = sc + lgot[k, :, first + R // 4 : first + R // 4 + 1].astype(F32)
                acc[r] = acc[r] + sc * dot(delta, cgot[k]) - inner * lgot[k].astype(F32)
    for i in range(1, S):
        j = peer(i)
        go(remote(ans.at[j], back.at[me], a_send.at[i], a_recv.at[me], on_section(j)))
    back[me] = ans[me]
    for i in range(1, S):
        j = peer(S - i)
        rows = pl.ds(pl.multiple_of(jnp.where(j < me, j, S - 1 - j) * R, R), R)
        lanes = pl.ds(pl.multiple_of(jnp.where(j < me, 0, T), T), T)
        remote(act_t.at[0], low.at[rows, lanes], t_send.at[i], t_recv.at[j], on_section(j)).wait_recv()
    lower = low[...].astype(F32)
    for i in range(1, S):
        j = peer(S - i)
        remote(ans.at[j], back.at[j], a_send.at[i], a_recv.at[j], on_section(j)).wait_recv()

    answer = back[...].reshape(T, 128)
    deltas = [answer[:, r * R : (r + 1) * R] for r in range(2)]
    turned = answer[:, 0 : 2 * R].astype(F32).T.astype(BF16)
    for r in range(2):
        tokens = slice(r * T, (r + 1) * T)
        seen = lower[:, tokens]
        tall = turned[r * R : (r + 1) * R].astype(F32) * pre_t[r * R : (r + 1) * R]
        sc = scale_t[0:1, tokens]
        pull = jnp.sum(tall, axis=0, keepdims=True) * (-1.0 / D) * (sc * sc)
        mix[:, tokens] = (seen * pull).astype(BF16)
        scaled = (deltas[r].astype(F32) * scale_v[tokens, 0:1]).astype(BF16)
        mix[:, 2 * T + r * R : 2 * T + (r + 1) * R] = dot(low[:, tokens], scaled).astype(BF16)
    W = min(512, CH)

    def terms(q):
        def part(i, carry):
            cols = pl.ds(pl.multiple_of(q * CH + i * W, W), W)
            below = dot(mix[...], lhs[:, cols]).astype(BF16)
            for j in range(S):
                for h in range(2):
                    es[h, j // 2, j % 2, :, cols] = below[j * R + h * H : j * R + (h + 1) * H]
            return carry

        lax.fori_loop(0, CH // W, part, 0)
        go(remote(
            es.at[1 - core, :, :, :, chunk(q)], pe.at[:, :, :, chunk(q)],
            c_send.at[q], c_recv.at[q], on_dp(mate),
        ))

    def down_terms(q):
        def part(i, carry):
            cols = pl.ds(pl.multiple_of(i * W, W), W)
            for r in range(2):
                rows = slice(r * T, (r + 1) * T)
                term = dot(turned[r * R : (r + 1) * R], hv[rows, cols]).astype(BF16)
                for h in range(2):
                    ds[h, r, :, cols] = term[h * H : (h + 1) * H]
            return carry

        lax.fori_loop(0, D // W, part, 0)
        go(remote(ds.at[1 - core], dr, d_send.at[0], d_recv.at[0], on_dp(mate)))

    def down_send(q):
        remote(dr, dr, d_send.at[0], d_recv.at[0], on_dp(mate)).wait_recv()
        dr[...] = (ds[core].astype(F32) + dr[...].astype(F32)).astype(BF16)
        go(remote(dr.at[1], fr, f_send.at[0], f_recv.at[0], on_section(mirror)))

    def step_y(q):
        landed = pe.at[:, :, :, chunk(q)]
        remote(landed, landed, c_send.at[q], c_recv.at[q], on_dp(mate)).wait_recv()
        ss[:, :, :, chunk(q)] = (
            es[core, :, :, :, chunk(q)].astype(F32) + pe[:, :, :, chunk(q)].astype(F32)
        ).astype(BF16)
        for way in range(2):
            go(remote(
                ss.at[:, 1 - yl, :, side(q, way)], yb.at[:, :, side(q, way)],
                ty_send.at[way, q], ty_recv.at[way, q], y_next(way),
            ))

    def step_x(q):
        for way in range(2):
            landed = yb.at[:, :, side(q, way)]
            remote(landed, landed, ty_send.at[way, q], ty_recv.at[way, q], y_next(way)).wait_recv()
        xs[:, :, chunk(q)] = (
            ss[:, yl, :, chunk(q)].astype(F32) + yb[:, :, chunk(q)].astype(F32)
        ).astype(BF16)
        for i in range(1, X):
            k = x_peer(i)
            go(remote(xs.at[k, :, chunk(q)], xr.at[x, :, chunk(q)], tx_send.at[i, q], tx_recv.at[x, q], in_row(k)))

    def step_z(q):
        for i in range(1, X):
            k = x_peer(X - i)
            landed = xr.at[k, :, chunk(q)]
            remote(landed, landed, tx_send.at[i, q], tx_recv.at[k, q], in_row(k)).wait_recv()
        if q == 0:
            remote(fr, fr, f_send.at[0], f_recv.at[0], on_section(mirror)).wait_recv()
            remote(own_r, own_r, o_send.at[0], o_recv.at[0], on_dp(mate)).wait_recv()
        whole = own_s[core, :, chunk(q)] + own_r[:, chunk(q)] + xs[x, :, chunk(q)].astype(F32)
        for k in range(X):
            whole = whole + xr[k, :, chunk(q)].astype(F32)
        zs[0:H, chunk(q)] = whole.astype(BF16)
        zs[H:R, chunk(q)] = (dr[0, :, chunk(q)].astype(F32) + fr[:, chunk(q)].astype(F32)).astype(BF16)
        for i in range(1, NZ):
            k = lax.rem(z + i, NZ)
            source = pl.ds(pl.multiple_of(q * CH + k * 128, 128), 128)
            go(remote(
                zs.at[:, source], zr.at[z, :, pl.ds(q * 128, 128)],
                z_send.at[i, q], z_recv.at[z, q], on_dp(place(yh, k)),
            ))
        zr[z, :, q * 128 : (q + 1) * 128] = zs[:, pl.ds(pl.multiple_of(q * CH + z * 128, 128), 128)]

    def y_copy(q, c):
        return remote(
            zt.at[q], yr.at[core, yh], y_send.at[c, q], y_recv.at[core, yh], on_dp(place(q, z, c))
        )

    def on_other(q, c, act):
        @pl.when((yh != q) | (core != c))
        def _():
            act()

    def step_yh(q):
        for i in range(1, NZ):
            k = lax.rem(z + NZ - i, NZ)
            landed = zr.at[k, :, pl.ds(q * 128, 128)]
            remote(landed, landed, z_send.at[i, q], z_recv.at[k, q], on_dp(place(yh, k))).wait_recv()
        whole = zr[0, :, q * 128 : (q + 1) * 128].astype(F32)
        for k in range(1, NZ):
            whole = whole + zr[k, :, q * 128 : (q + 1) * 128].astype(F32)
        zt[q] = whole

        for c in range(CORES):
            on_other(q, c, lambda: y_copy(q, c).start())

        @pl.when(yh == q)
        def _():
            yr[core, q] = zt[q]

    steps = [(terms, 0.0), (step_y, 1.1), (step_x, 3.4), (step_z, 5.6), (step_yh, 7.8)]
    order = [(q + late_by, step, q) for step, late_by in steps for q in range(NY)]
    order += [(1.3, down_terms, 0), (2.1, down_send, 0)]
    for _, step, q in sorted(order, key=lambda entry: entry[0]):
        step(q)

    for c in range(CORES):
        for k in range(NY):
            landed = yr.at[c, k]
            copy = remote(landed, landed, y_send.at[c, k], y_recv.at[c, k], on_dp(place(k, z, c)))
            on_other(k, c, copy.wait_recv)
    for c in range(CORES):
        whole = yr[c, 0]
        for k in range(1, NY):
            whole = whole + yr[c, k]
        out[c] = whole

    for copy in sent:
        copy.wait_send()
    for q in range(NY):
        for c in range(CORES):
            on_other(q, c, y_copy(q, c).wait_send)


def own_columns(parts, out_in, out_out):
    core = lax.rem(lax.axis_index("dp"), CORES)
    H = parts.shape[1] // 2
    for h in range(2):
        chosen = jnp.where(core == 0, parts[h, :, :64], parts[h, :, 64:])
        out_out[h * H : (h + 1) * H, :] = chosen[:H]
        out_in[h * H : (h + 1) * H, :] = chosen[H:]


def on_device(rings, saved, top_grad, gains, adapter_in, adapter_out):
    S = lax.axis_size("section")
    NY, NZ = rings
    _, _, T, D = saved.shape
    R = adapter_in.shape[3]
    X, NL, H, Q = S // 2, S * R, R // 2, T // S
    dma = pltpu.SemaphoreType.DMA
    scratch = [
        pltpu.VMEM((2 * T + 2 * R, D), BF16),
        pltpu.VMEM((2 * T, D), BF16),
        pltpu.VMEM((2 * T, D), BF16),
        pltpu.VMEM((2, D), F32),
        pltpu.VMEM((2, R, D), BF16),
        pltpu.VMEM((2, R, D), BF16),
        pltpu.VMEM((X, 2, R, D), BF16),
        pltpu.VMEM((2 * T, 128), F32),
        pltpu.VMEM((8, 2 * T), F32),
        pltpu.VMEM((T, 2 * R), F32),
        pltpu.VMEM((2 * R, T), F32),
        pltpu.VMEM((NL, 2 * T + 2 * R), BF16),
        pltpu.VMEM((T, 4 * R), F32),
        pltpu.VMEM((T, NL), BF16),
        pltpu.VMEM((R, NL), BF16),
        pltpu.VMEM((S, Q, 4 * R), F32),
        pltpu.VMEM((S, Q, NL), BF16),
        pltpu.VMEM((S, R, NL), BF16),
        pltpu.VMEM((2, R, T), BF16),
        pltpu.VMEM((NL, 2 * T), BF16),
        pltpu.VMEM((R, 2 * T), BF16),
        pltpu.VMEM((S, Q, 128), BF16),
        pltpu.VMEM((S, Q, 128), BF16),
        pltpu.VMEM((2, H, D), F32),
        pltpu.VMEM((H, D), F32),
        pltpu.VMEM((2, 2, H, D), BF16),
        pltpu.VMEM((2, H, D), BF16),
        pltpu.VMEM((2, X, 2, H, D), BF16),
        pltpu.VMEM((X, 2, H, D), BF16),
        pltpu.VMEM((X, 2, H, D), BF16),
        pltpu.VMEM((X, H, D), BF16),
        pltpu.VMEM((X, H, D), BF16),
        pltpu.VMEM((X, H, D), BF16),
        pltpu.VMEM((H, D), BF16),
        pltpu.VMEM((R, D), BF16),
        pltpu.VMEM((NZ, R, NY * 128), BF16),
        pltpu.VMEM((NY, R, 128), F32),
        pltpu.VMEM((CORES, NY, R, 128), F32),
        dma((8,)),
    ]
    scratch += [dma((X,))] * 2 + [dma((S,))] * 2 + [dma((2,))] * 2 + [dma((3,))] * 2
    scratch += [dma((S,))] * 4 + [dma((1,))] * 2 + [dma((S,))] * 4
    scratch += [dma((S,))] * 2 + [dma((1,))] * 4 + [dma((NY,))] * 2 + [dma((2, NY))] * 2
    scratch += [dma((X, NY))] * 2 + [dma((1,))] * 2
    scratch += [dma((NZ, NY))] * 2 + [dma((CORES, NY))] * 2
    half = D // (NY * NZ * CORES)
    vmem = pl.BlockSpec(memory_space=pltpu.VMEM)
    parts = pl.pallas_call(
        partial(kernel, (S, NY, NZ, T, D, R)),
        out_shape=jax.ShapeDtypeStruct((2, R, 128), F32),
        in_specs=[pl.BlockSpec(memory_space=pl.ANY)] * 5,
        out_specs=vmem,
        scratch_shapes=scratch,
        compiler_params=pltpu.CompilerParams(
            collective_id=0, has_side_effects=True, vmem_limit_bytes=56 * 2**20
        ),
        cost_estimate=pl.CostEstimate(
            flops=4 * 10**9, bytes_accessed=6 * 2**20, transcendentals=2 * T * R
        ),
    )(saved, top_grad, gains, jnp.swapaxes(adapter_in, 2, 3), adapter_out)
    shape = jax.ShapeDtypeStruct((R, half), F32)
    grad_in, grad_out = pl.pallas_call(
        own_columns, out_shape=(shape, shape), in_specs=[vmem], out_specs=(vmem, vmem)
    )(parts)
    return (grad_in.T[None], grad_out[None])


def solution(mesh):
    in_specs = (
        P("section", None, "dp", None),
        P(None, "dp", None),
        P("section", None, None),
        P("section", None, None, None),
        P("section", None, None, None),
    )
    out_specs = (P("section", "dp", None), P("section", None, "dp"))
    return jax.shard_map(
        partial(on_device, RINGS[mesh.shape["dp"]]),
        mesh=mesh, in_specs=in_specs, out_specs=out_specs, check_vma=False,
    )
```

time: 1020 us -> 72.5 us (0.07); the launches traced: 1010 us -> 72.3 us
  waiting for transfers between devices: 791 us -> 0 us
  starting transfers between devices: 76.8 us -> 0 us
  Pallas kernels: 0 us -> 71.7 us
  local copies, waits for them, and re-layouts: 62.5 us -> 0 us
  other arithmetic: 48.3 us -> 0 us
  between operations: 14 us -> 0.64 us
  matrix products: 12.6 us -> 0 us
    unnamed x8 -> x0, waiting for transfers between devices: 594 us -> none
    ppermute x20 -> x0, waiting for transfers between devices: 197 us -> none  [the longest x14 196 us: passed_along(): return lax.ppermute(shard, axis, pairs)]
    ppermute x20 -> x0, starting transfers between devices: 76.6 us -> none  [the longest x14 56 us: passed_along(): return lax.ppermute(shard, axis, pairs)]
    pallas_call x0 -> x2, Pallas kernels: none -> 71.7 us  [the longest x1 70.2 us: on_device(): pl.pallas_call(partial(kernel, (S, NY, NZ, T, D, R)), out_shape=jax.Shape...]
    add x18 -> x0, other arithmetic: 41.9 us -> none  [the longest x9 21.1 us: advance(): sums[2 * replica] = sums[2 * replica] + term_in]
    cond x20 -> x0, local copies, waits for them, and re-layouts: 19.8 us -> none
    broadcast_in_dim x28 -> x0, local copies, waits for them, and re-layouts: 18.3 us -> none  [the longest x14 11.2 us: on_device(): zero_out = jnp.zeros((rank, width), jnp.float32)]
    unnamed x23 -> x0, local copies, waits for them, and re-layouts: 15.8 us -> none
  transfers between devices with their start and end apart: 24 -> 0, of which waited for: 19 -> 0; matrix products, arithmetic and copies ran while one was open for 7% -> 0% of each run, Pallas kernels for 0% -> 0%
where the time goes in v2:
time: 72.5 us; the launch traced here: 72.3 us
  Pallas kernels  71.7 us (99%)
    pallas_call x1, Pallas kernels, on_device(): pl.pallas_call(partial(kernel, (S, NY, NZ, T, D, R)), out_shape=jax.Shape...  70.2 us

profile of v2, /device:TPU:57, one launch (start us, length us, event | category | flops | bytes accessed | tf_op | source)
XLA Modules:
  0.0 72.3 jit_solution(14250049547895009092)
XLA Ops:
  0.6 70.2 %shard_map.68.parts = f32[2,32,128]{2,1,0:T(8,128)} custom-call(bf16[1,2,128,4096]{3,2,1,0:T(8,128)(2,1)} %saved.1, bf16[2,128,4096]{2,1,0:T(8,128)(2,1)} %top.1, f32[1,2,4096]{2,1,0:T(2,128)} %gains.1, bf16[1,2,32,4096]{3,2,1,0:T(8,128)(2,1)} %bitcast.5, bf16[1,2,32,4096]{3,2,1,0:T(8,128)(2,1)} %wout.1), custom_call_target="tpu_custom_call" | custom-call | flops 4000000000 | bytes 6291456 | tf_op jit(solution)/shard_map/pallas_call | solution.py:552
  70.9 1.4 %shard_map.69 = (f32[32,64]{1,0:T(8,128)}, f32[32,64]{1,0:T(8,128)}) custom-call(f32[2,32,128]{2,1,0:T(8,128)} %shard_map.68.parts), custom_call_target="tpu_custom_call" | custom-call | tf_op jit(solution)/shard_map/pallas_call | solution.py:566

commit v3 on v2

--- a/solution.py
+++ b/solution.py
@@ -26,7 +26,7 @@
     dims, saved, top, gains, win, wout, out,
     lhs, tv, hv, gv, iv, ov, wall, scale_v, scale_t, pre_v, pre_t, mix, early, late, coup, egot, lgot, cgot,
     act_t, low, same, ans, back, own_s, own_r, ds, dr, es, pe, ss, yb, xs, xr, fr, zs, zr, zt, yr,
-    load_sem, wx_send, wx_recv, wd_send, wd_recv, wy_send, wy_recv, wc_send, wc_recv,
+    load_sem, wx_send, wx_recv, wd_send, wd_recv, wy_send, wy_recv, wz_send, wz_recv, wc_send, wc_recv,
     e_send, e_recv, t_send, t_recv, g_send, g_recv, v_send, v_recv, k_send, k_recv,
     a_send, a_recv, o_send, o_recv, d_send, d_recv, c_send, c_recv, ty_send, ty_recv, tx_send, tx_recv, f_send, f_recv,
     z_send, z_recv, y_send, y_recv,
@@ -96,8 +96,17 @@
     def section_at(dx, dy, sign=1):
         return 2 * lax.rem(x + X + sign * dx, X) + (1 - yl if dy else yl)
 
-    own_unit = pltpu.make_async_copy(wout.at[0, yl, half], wall.at[x, yl, half], load_sem.at[7])
-    own_unit.start()
+    near = pl.ds(0, D // 2)
+    E = D // 4
+    odd = lax.rem(z, 2)
+    mine_z = pl.ds(pl.multiple_of(D // 2 + odd * E, E), E)
+    theirs_z = pl.ds(pl.multiple_of(D // 2 + (1 - odd) * E, E), E)
+    own_units = [
+        pltpu.make_async_copy(wout.at[0, yl, half, cols], wall.at[x, yl, half, cols], load_sem.at[7 + n])
+        for n, cols in enumerate((near, mine_z))
+    ]
+    for copy in own_units:
+        copy.start()
 
     loads = []
     for r in range(2):
@@ -121,30 +130,20 @@
         pl.semaphore_signal(barrier, inc=1, device_id=device, device_id_type=pl.DeviceIdType.MESH)
     pl.semaphore_wait(barrier, len(greeted))
 
-    near = pl.ds(0, D // 2)
-    rest = pl.ds(D // 2, D // 2)
-
     def upper(j):
         return jnp.where(j > me, 0, 1)
 
-    rows_sent = []
     for i in range(1, X):
         j = 2 * x_peer(i) + yl
-        copy = remote(
+        go(remote(
             wout.at[0, upper(j), half, near], wall.at[x, yl, half, near], wx_send.at[i], wx_recv.at[x], on_section(j)
-        )
-        copy.start()
-        rows_sent.append(copy)
-
-    def send_direct():
-        for copy in rows_sent:
-            copy.wait_send()
-        for n, (dx, dy) in reversed(list(enumerate(steps_of))):
-            j = section_at(dx, dy)
-            go(remote(
-                wout.at[0, upper(j), half, rest], wall.at[x, yl, half, rest],
-                wd_send.at[n], wd_recv.at[me], on_section(j),
-            ))
+        ))
+    for n, (dx, dy) in reversed(list(enumerate(steps_of))):
+        j = section_at(dx, dy)
+        go(remote(
+            wout.at[0, upper(j), half, mine_z], wall.at[x, yl, half, mine_z],
+            wd_send.at[n], wd_recv.at[me], on_section(j),
+        ))
 
     for j in range(S):
         @pl.when(j >= me)
@@ -158,10 +157,16 @@
     xr[x] = jnp.zeros((H, D), BF16)
 
     def onward(way):
-        return pl.ds(way * (D // 4), D // 4)
+        return pl.ds(way * E, E)
+
+    def onward_z(way, parity):
+        return pl.ds(pl.multiple_of(D // 2 + parity * E + way * (E // 2), E // 2), E // 2)
+
+    def z_next(way):
+        return on_dp(place(yh, lax.rem(z + (1 if way == 0 else NZ - 1), NZ)))
 
     def gather_row():
-        own_unit.wait()
+        own_units[0].wait()
         for i in range(1, X):
             k = x_peer(X - i)
             landed = wall.at[k, yl, half, near]
@@ -172,30 +177,42 @@
         row = wall.at[:, yl, half, near]
         go(remote(row, row, wc_send.at[0], wc_recv.at[0], on_dp(mate)))
 
+    def gather_direct():
+        own_units[1].wait()
+        for n, (dx, dy) in enumerate(steps_of):
+            j = section_at(dx, dy, -1)
+            landed = wall.at[j // 2, lax.rem(j, 2), half, mine_z]
+            remote(landed, landed, wd_send.at[n], wd_recv.at[j], on_section(j)).wait_recv()
+        for way in range(2):
+            part = wall.at[:, :, half, onward_z(way, odd)]
+            go(remote(part, part, wz_send.at[way], wz_recv.at[way], z_next(way)))
+        part = wall.at[:, :, half, mine_z]
+        go(remote(part, part, wc_send.at[1], wc_recv.at[1], on_dp(mate)))
+
     def gather_y():
         for way in range(2):
             row = wall.at[:, 1 - yl, half, onward(way)]
             remote(row, row, wy_send.at[way], wy_recv.at[way], y_next(way)).wait_recv()
         row = wall.at[:, 1 - yl, half, near]
-        go(remote(row, row, wc_send.at[1], wc_recv.at[1], on_dp(mate)))
-
-    def gather_direct():
-        for n, (dx, dy) in enumerate(steps_of):
-            j = section_at(dx, dy, -1)
-            landed = wall.at[j // 2, lax.rem(j, 2), half, rest]
-            remote(landed, landed, wd_send.at[n], wd_recv.at[j], on_section(j)).wait_recv()
-        row = wall.at[:, :, half, rest]
         go(remote(row, row, wc_send.at[2], wc_recv.at[2], on_dp(mate)))
 
+    def gather_z():
+        for way in range(2):
+            part = wall.at[:, :, half, onward_z(way, 1 - odd)]
+            remote(part, part, wz_send.at[way], wz_recv.at[way], z_next(way)).wait_recv()
+        part = wall.at[:, :, half, theirs_z]
+        go(remote(part, part, wc_send.at[3], wc_recv.at[3], on_dp(mate)))
+
     def project_near():
-        for n, line in enumerate((yl, 1 - yl)):
+        for n, line in ((0, yl), (2, 1 - yl)):
             row = wall.at[:, line, other_half, near]
             remote(row, row, wc_send.at[n], wc_recv.at[n], on_dp(mate)).wait_recv()
         return over_last(lhs[:, : D // 2], wall[:, :, :, : D // 2].reshape(NL, D // 2))
 
     def project_rest():
-        row = wall.at[:, :, other_half, rest]
-        remote(row, row, wc_send.at[2], wc_recv.at[2], on_dp(mate)).wait_recv()
+        for n, cols in ((1, mine_z), (3, theirs_z)):
+            part = wall.at[:, :, other_half, cols]
+            remote(part, part, wc_send.at[n], wc_recv.at[n], on_dp(mate)).wait_recv()
         return over_last(lhs[:, D // 2 :], wall[:, :, :, D // 2 :].reshape(NL, D // 2))
 
     def piece_norm():
@@ -262,13 +279,13 @@
         egot[me] = early[pl.ds(pl.multiple_of(me * Q, Q), Q), :]
 
     piece_norm()
-    send_direct()
     piece_hidden()
     gather_row()
+    gather_direct()
     piece_down()
     piece_up()
     gather_y()
-    gather_direct()
+    gather_z()
     across = project_near() + project_rest()
 
     block = lax.broadcasted_iota(jnp.int32, (R, NL), 1) // R
@@ -461,9 +478,9 @@
         def _():
             yr[core, q] = zt[q]
 
-    steps = [(terms, 0.0), (step_y, 1.1), (step_x, 3.4), (step_z, 5.6), (step_yh, 7.8)]
+    steps = [(terms, 0.0), (step_y, 1.1), (step_x, 3.9), (step_z, 6.9), (step_yh, 9.9)]
     order = [(q + late_by, step, q) for step, late_by in steps for q in range(NY)]
-    order += [(1.3, down_terms, 0), (2.1, down_send, 0)]
+    order += [(0.5, down_terms, 0), (1.15, down_send, 0)]
     for _, step, q in sorted(order, key=lambda entry: entry[0]):
         step(q)
 
@@ -540,9 +557,9 @@
         pltpu.VMEM((NZ, R, NY * 128), BF16),
         pltpu.VMEM((NY, R, 128), F32),
         pltpu.VMEM((CORES, NY, R, 128), F32),
-        dma((8,)),
+        dma((9,)),
     ]
-    scratch += [dma((X,))] * 2 + [dma((S,))] * 2 + [dma((2,))] * 2 + [dma((3,))] * 2
+    scratch += [dma((X,))] * 2 + [dma((S,))] * 2 + [dma((2,))] * 4 + [dma((4,))] * 2
     scratch += [dma((S,))] * 4 + [dma((1,))] * 2 + [dma((S,))] * 4
     scratch += [dma((S,))] * 2 + [dma((1,))] * 4 + [dma((NY,))] * 2 + [dma((2, NY))] * 2
     scratch += [dma((X, NY))] * 2 + [dma((1,))] * 2

time: 72.5 us -> 71 us (0.979)
  Pallas kernels: 71.7 us -> 70 us
    pallas_call x1, Pallas kernels: 70.2 us -> 68.6 us  [on_device(): pl.pallas_call(partial(kernel, (S, NY, NZ, T, D, R)), out_shape=jax.Shape...]
where the time goes in v3:
time: 71 us; the launch traced here: 70.7 us
  Pallas kernels  70 us (99%)
    pallas_call x1, Pallas kernels, on_device(): pl.pallas_call(partial(kernel, (S, NY, NZ, T, D, R)), out_shape=jax.Shape...  68.6 us
    pallas_call x1, Pallas kernels, on_device(): pl.pallas_call(own_columns, out_shape=(shape, shape), in_specs=[vmem], ou...  1.44 us

profile of v3, /device:TPU:57, one launch (start us, length us, event | category | flops | bytes accessed | tf_op | source)
XLA Modules:
  0.0 70.7 jit_solution(12539082284912083523)
XLA Ops:
  0.6 68.6 %shard_map.68.parts = f32[2,32,128]{2,1,0:T(8,128)} custom-call(bf16[1,2,128,4096]{3,2,1,0:T(8,128)(2,1)} %saved.1, bf16[2,128,4096]{2,1,0:T(8,128)(2,1)} %top.1, f32[1,2,4096]{2,1,0:T(2,128)} %gains.1, bf16[1,2,32,4096]{3,2,1,0:T(8,128)(2,1)} %bitcast.5, bf16[1,2,32,4096]{3,2,1,0:T(8,128)(2,1)} %wout.1), custom_call_target="tpu_custom_call" | custom-call | flops 4000000000 | bytes 6291456 | tf_op jit(solution)/shard_map/pallas_call | solution.py:569
  69.2 1.4 %shard_map.69 = (f32[32,64]{1,0:T(8,128)}, f32[32,64]{1,0:T(8,128)}) custom-call(f32[2,32,128]{2,1,0:T(8,128)} %shard_map.68.parts), custom_call_target="tpu_custom_call" | custom-call | tf_op jit(solution)/shard_map/pallas_call | solution.py:583

commit v4 on v3

--- a/solution.py
+++ b/solution.py
@@ -96,6 +96,14 @@
     def section_at(dx, dy, sign=1):
         return 2 * lax.rem(x + X + sign * dx, X) + (1 - yl if dy else yl)
 
+    barrier = pltpu.get_barrier_semaphore()
+    greeted = [on_section(peer(i)) for i in range(1, S)] + [on_dp(mate)]
+    greeted += [{"section": beside, "dp": place(far, z)}]
+    greeted += [on_dp(place(yh, lax.rem(z + i, NZ))) for i in range(1, NZ)]
+    greeted += [on_dp(place(lax.rem(yh + i, NY), z, c)) for i in range(1, NY) for c in range(CORES)]
+    for device in greeted:
+        pl.semaphore_signal(barrier, inc=1, device_id=device, device_id_type=pl.DeviceIdType.MESH)
+
     near = pl.ds(0, D // 2)
     E = D // 4
     odd = lax.rem(z, 2)
@@ -121,13 +129,6 @@
     for copy in loads:
         copy.start()
 
-    barrier = pltpu.get_barrier_semaphore()
-    greeted = [on_section(peer(i)) for i in range(1, S)] + [on_dp(mate)]
-    greeted += [{"section": beside, "dp": place(far, z)}]
-    greeted += [on_dp(place(yh, lax.rem(z + i, NZ))) for i in range(1, NZ)]
-    greeted += [on_dp(place(lax.rem(yh + i, NY), z, c)) for i in range(1, NY) for c in range(CORES)]
-    for device in greeted:
-        pl.semaphore_signal(barrier, inc=1, device_id=device, device_id_type=pl.DeviceIdType.MESH)
     pl.semaphore_wait(barrier, len(greeted))
 
     def upper(j):
@@ -209,11 +210,10 @@
             remote(row, row, wc_send.at[n], wc_recv.at[n], on_dp(mate)).wait_recv()
         return over_last(lhs[:, : D // 2], wall[:, :, :, : D // 2].reshape(NL, D // 2))
 
-    def project_rest():
-        for n, cols in ((1, mine_z), (3, theirs_z)):
-            part = wall.at[:, :, other_half, cols]
-            remote(part, part, wc_send.at[n], wc_recv.at[n], on_dp(mate)).wait_recv()
-        return over_last(lhs[:, D // 2 :], wall[:, :, :, D // 2 :].reshape(NL, D // 2))
+    def project_rest(n, cols):
+        part = wall.at[:, :, other_half, cols]
+        remote(part, part, wc_send.at[n], wc_recv.at[n], on_dp(mate)).wait_recv()
+        return over_last(lhs[:, cols], wall[:, :, :, cols].reshape(NL, E))
 
     def piece_norm():
         for n in range(2):
@@ -284,9 +284,11 @@
     gather_direct()
     piece_down()
     piece_up()
+    across = project_rest(1, mine_z)
     gather_y()
     gather_z()
-    across = project_near() + project_rest()
+    across = across + project_near()
+    across = across + project_rest(3, theirs_z)
 
     block = lax.broadcasted_iota(jnp.int32, (R, NL), 1) // R
     coup[...] = jnp.where(
@@ -478,7 +480,7 @@
         def _():
             yr[core, q] = zt[q]
 
-    steps = [(terms, 0.0), (step_y, 1.1), (step_x, 3.9), (step_z, 6.9), (step_yh, 9.9)]
+    steps = [(terms, 0.0), (step_y, 1.1), (step_x, 3.9), (step_z, 6.4), (step_yh, 9.4)]
     order = [(q + late_by, step, q) for step, late_by in steps for q in range(NY)]
     order += [(0.5, down_terms, 0), (1.15, down_send, 0)]
     for _, step, q in sorted(order, key=lambda entry: entry[0]):

time: 71 us -> 70.7 us (level)
  no operation moved by 1% of the time
where the time goes in v4:
time: 70.7 us; the launch traced here: 70.5 us
  Pallas kernels  69.9 us (99%)
    pallas_call x1, Pallas kernels, on_device(): pl.pallas_call(partial(kernel, (S, NY, NZ, T, D, R)), out_shape=jax.Shape...  68.4 us
    pallas_call x1, Pallas kernels, on_device(): pl.pallas_call(own_columns, out_shape=(shape, shape), in_specs=[vmem], ou...  1.44 us

profile of v4, /device:TPU:57, one launch (start us, length us, event | category | flops | bytes accessed | tf_op | source)
XLA Modules:
  0.0 70.5 jit_solution(4973650769116650263)
XLA Ops:
  0.6 68.4 %shard_map.68.parts = f32[2,32,128]{2,1,0:T(8,128)} custom-call(bf16[1,2,128,4096]{3,2,1,0:T(8,128)(2,1)} %saved.1, bf16[2,128,4096]{2,1,0:T(8,128)(2,1)} %top.1, f32[1,2,4096]{2,1,0:T(2,128)} %gains.1, bf16[1,2,32,4096]{3,2,1,0:T(8,128)(2,1)} %bitcast.5, bf16[1,2,32,4096]{3,2,1,0:T(8,128)(2,1)} %wout.1), custom_call_target="tpu_custom_call" | custom-call | flops 4000000000 | bytes 6291456 | tf_op jit(solution)/shard_map/pallas_call | solution.py:571
  69.1 1.4 %shard_map.69 = (f32[32,64]{1,0:T(8,128)}, f32[32,64]{1,0:T(8,128)}) custom-call(f32[2,32,128]{2,1,0:T(8,128)} %shard_map.68.parts), custom_call_target="tpu_custom_call" | custom-call | tf_op jit(solution)/shard_map/pallas_call | solution.py:585

commit v5 on v4

--- a/solution.py
+++ b/solution.py
@@ -101,7 +101,7 @@
     greeted += [{"section": beside, "dp": place(far, z)}]
     greeted += [on_dp(place(yh, lax.rem(z + i, NZ))) for i in range(1, NZ)]
     greeted += [on_dp(place(lax.rem(yh + i, NY), z, c)) for i in range(1, NY) for c in range(CORES)]
-    for device in greeted:
+    for device in reversed(greeted):
         pl.semaphore_signal(barrier, inc=1, device_id=device, device_id_type=pl.DeviceIdType.MESH)
 
     near = pl.ds(0, D // 2)

time: 70.7 us -> 70.7 us (level)
  no operation moved by 1% of the time
where the time goes in v5:
time: 70.7 us; the launch traced here: 70.5 us
  Pallas kernels  69.9 us (99%)
    pallas_call x1, Pallas kernels, on_device(): pl.pallas_call(partial(kernel, (S, NY, NZ, T, D, R)), out_shape=jax.Shape...  68.4 us
    pallas_call x1, Pallas kernels, on_device(): pl.pallas_call(own_columns, out_shape=(shape, shape), in_specs=[vmem], ou...  1.44 us

profile of v5, /device:TPU:57, one launch (start us, length us, event | category | flops | bytes accessed | tf_op | source)
XLA Modules:
  0.0 70.5 jit_solution(5223961739645861925)
XLA Ops:
  0.6 68.4 %shard_map.68.parts = f32[2,32,128]{2,1,0:T(8,128)} custom-call(bf16[1,2,128,4096]{3,2,1,0:T(8,128)(2,1)} %saved.1, bf16[2,128,4096]{2,1,0:T(8,128)(2,1)} %top.1, f32[1,2,4096]{2,1,0:T(2,128)} %gains.1, bf16[1,2,32,4096]{3,2,1,0:T(8,128)(2,1)} %bitcast.5, bf16[1,2,32,4096]{3,2,1,0:T(8,128)(2,1)} %wout.1), custom_call_target="tpu_custom_call" | custom-call | flops 4000000000 | bytes 6291456 | tf_op jit(solution)/shard_map/pallas_call | solution.py:571
  69.1 1.4 %shard_map.69 = (f32[32,64]{1,0:T(8,128)}, f32[32,64]{1,0:T(8,128)}) custom-call(f32[2,32,128]{2,1,0:T(8,128)} %shard_map.68.parts), custom_call_target="tpu_custom_call" | custom-call | tf_op jit(solution)/shard_map/pallas_call | solution.py:585
